TPU v7x, 256 devices: a whole 4x4x8 slice. The times are simulated.
256 devices in a mesh: grp: 16 (over x, y), chan: 16 (over z, core).
Axes of the slice: x: 4, y: 4, z: 8, core: 2. Of those that a mesh axis runs over, the one named last changes fastest.
Arguments:
- visibilities: float32 [2, 1536, 32768], P(None, 'chan', 'grp'), may hold values from -7 to 7
- baseline_antennas: int32 [2, 32768], P(None, 'grp'), may hold values from 0 to 349, as said below
- group_ids: int32 [16, 2048], P('grp'), may hold values from 0 to 127, as said below
- sky_model: float32 [2, 1536, 2048], P(None, 'chan', 'grp'), may hold values from -4 to 4
- starting_gain_values: float32 [2, 1536, 350], P(None, 'chan'), may hold values from 0.6 to 1.4
- antenna_coordinates: float32 [2, 350], replicated, may hold values from -1 to 1
Outputs:
- gains: float32 [2, 1536, 350], P(None, 'chan')
- calibrated: float32 [2, 1536, 2048], P(None, 'chan', 'grp')
- chi_square: float32 [1536], P('chan')
Inputs may be any that keep to these rules, and one draw needn't show every extreme that they name: `baseline_antennas`: the two antennas of a baseline differ. `group_ids`: each row holds the baselines of one index of grp; ids never fall along a row, start at 0, and each of the 128 ids names one or more baselines.
All inputs are finite; a program needn't handle non-finite values.
Results may differ from a plain program's by a relative error of at most 0.0001.
Values sent between devices are 32-bit elements; how exact they have to be, the bound alone decides.
A program may use at most 256 MiB of HBM per device.

v0:
```python
import jax
import jax.numpy as jnp
from jax import lax
from jax.sharding import PartitionSpec as P

CHANNEL_COUNT = 1536
NDLY = 64
ITERS = 4


highest = lax.Precision.HIGHEST
ridge_term = 0.5
epsilon = 1e-06


def conjugated_value(number):
    return jnp.stack([number[0], -number[1]])


def complex_product(former, latter):
    return jnp.stack(
        [
            former[0] * latter[0] - former[1] * latter[1],
            former[0] * latter[1] + former[1] * latter[0],
        ]
    )


def absolute_size(number):
    return number[0] * number[0] + number[1] * number[1]


def onehot_rows(indices, number):
    return (jnp.arange(number, dtype=jnp.int32)[:, None] == indices[None, :]).astype(jnp.float32)


def spread(source, lookup):
    return jnp.einsum("acn,nb->acb", source, lookup, precision=highest)


def collect(source, lookup):
    return jnp.einsum("acb,nb->acn", source, lookup, precision=highest)


def collect_real(source, lookup):
    return jnp.einsum("cb,nb->cn", source, lookup, precision=highest)


def delay_tables(number, band_size, mode_count):
    channel_ids = jnp.arange(number, dtype=jnp.int32)
    turn_counts = (
        channel_ids[:, None]
        * (jnp.arange(mode_count, dtype=jnp.int32)[None, :] - mode_count // 2)
        % band_size
    )
    angles = 2.0 * jnp.pi / band_size * turn_counts.astype(jnp.float32)
    frequency = 1.0 + channel_ids.astype(jnp.float32) / band_size
    return (jnp.cos(angles), jnp.sin(angles), frequency)


def delay_coefficients(cross_ratio, cosines, sine_table):
    real_part = (
        jnp.einsum("fk,fj->jk", cross_ratio[0], cosines, precision=highest)
        + jnp.einsum("fk,fj->jk", cross_ratio[1], sine_table, precision=highest)
    ) / CHANNEL_COUNT
    imag_part = (
        jnp.einsum("fk,fj->jk", cross_ratio[1], cosines, precision=highest)
        - jnp.einsum("fk,fj->jk", cross_ratio[0], sine_table, precision=highest)
    ) / CHANNEL_COUNT
    return (real_part, imag_part)


def smooth_phase(real_part, imag_part, cosines, sine_table):
    return jnp.einsum("jk,fj->fk", imag_part, cosines, precision=highest) + jnp.einsum(
        "jk,fj->fk", real_part, sine_table, precision=highest
    )


def channel_sums(unique, sky_part, phases, vectors):
    model_power = absolute_size(sky_part)
    squared = model_power * model_power
    east_part = vectors[0][None, :]
    north_part = vectors[1][None, :]
    return jnp.stack(
        [
            jnp.sum(absolute_size(unique), axis=1),
            jnp.sum(model_power, axis=1),
            jnp.sum(squared * east_part * east_part, axis=1),
            jnp.sum(squared * east_part * north_part, axis=1),
            jnp.sum(squared * north_part * north_part, axis=1),
            jnp.sum(model_power * phases * east_part, axis=1),
            jnp.sum(model_power * phases * north_part, axis=1),
        ]
    )


def solve_pair(entry_xx, entry_xy, entry_yy, right_x, right_y):
    ridge_shift = 0.001 * (entry_xx + entry_yy) + epsilon
    diag_first = entry_xx + ridge_shift
    diag_second = entry_yy + ridge_shift
    determinant = diag_first * diag_second - entry_xy * entry_xy
    return (
        (diag_second * right_x - entry_xy * right_y) / determinant,
        (diag_first * right_y - entry_xy * right_x) / determinant,
    )


def slope_terms(totals, frequency):
    squared = frequency * frequency
    return jnp.stack(
        [
            jnp.sum(squared * totals[2]),
            jnp.sum(squared * totals[3]),
            jnp.sum(squared * totals[4]),
            jnp.sum(frequency * totals[5]),
            jnp.sum(frequency * totals[6]),
        ]
    )


def slope_fit(terms):
    east_part, north_part = solve_pair(terms[0], terms[1], terms[2], terms[3], terms[4])
    return jnp.stack([east_part, north_part])


def apply_fit(unique, totals, frequency, delay_slope, vectors):
    amplitude = jnp.sqrt((totals[0] + epsilon) / (totals[1] + epsilon))
    tilt_east, tilt_north = solve_pair(totals[2], totals[3], totals[4], totals[5], totals[6])
    tilt_east = tilt_east - frequency * delay_slope[0]
    tilt_north = tilt_north - frequency * delay_slope[1]
    along_slope = delay_slope[0] * vectors[0] + delay_slope[1] * vectors[1]
    phase_turn = (
        frequency[:, None] * along_slope[None, :]
        + tilt_east[:, None] * vectors[0][None, :]
        + tilt_north[:, None] * vectors[1][None, :]
    )
    rotation_cos = jnp.cos(phase_turn)
    rotation_sin = jnp.sin(phase_turn)
    scale_back = 1.0 / amplitude[:, None]
    return jnp.stack(
        [
            (unique[0] * rotation_cos + unique[1] * rotation_sin) * scale_back,
            (unique[1] * rotation_cos - unique[0] * rotation_sin) * scale_back,
        ]
    )


def unique_fit(visibilities, leading_gain, trailing_gain, group_hot):
    weights = complex_product(leading_gain, conjugated_value(trailing_gain))
    update_numerator = collect(complex_product(visibilities, conjugated_value(weights)), group_hot)
    update_denominator = collect_real(absolute_size(weights), group_hot) + ridge_term
    return (update_numerator / update_denominator[None], weights)


def per_device(
    visibilities, baseline_antennas, group_ids, sky_model, starting_gain_values, antenna_coordinates
):
    antennas = starting_gain_values.shape[2]
    groups_here = sky_model.shape[2]
    first_hot = onehot_rows(baseline_antennas[0], antennas)
    second_hot = onehot_rows(baseline_antennas[1], antennas)
    group_hot = onehot_rows(group_ids[0], groups_here)
    current_gain = starting_gain_values
    for iteration in range(ITERS):
        leading_gain = spread(current_gain, first_hot)
        trailing_gain = spread(current_gain, second_hot)
        unique, weights = unique_fit(visibilities, leading_gain, trailing_gain, group_hot)
        unique_rows = spread(unique, group_hot)
        first_axis_share = complex_product(conjugated_value(trailing_gain), unique_rows)
        second_axis_share = complex_product(leading_gain, unique_rows)
        update_numerator = collect(
            complex_product(conjugated_value(first_axis_share), visibilities), first_hot
        ) + collect(complex_product(second_axis_share, conjugated_value(visibilities)), second_hot)
        update_denominator = collect_real(
            absolute_size(first_axis_share), first_hot
        ) + collect_real(absolute_size(second_axis_share), second_hot)
        update_numerator, update_denominator = lax.psum(
            (update_numerator, update_denominator), "grp"
        )
        current_gain = 0.5 * current_gain + 0.5 * update_numerator / (
            update_denominator[None] + ridge_term
        )
    leading_gain = spread(current_gain, first_hot)
    trailing_gain = spread(current_gain, second_hot)
    unique, weights = unique_fit(visibilities, leading_gain, trailing_gain, group_hot)
    misfit = visibilities - complex_product(weights, spread(unique, group_hot))
    chi_square = lax.psum(jnp.sum(absolute_size(misfit), axis=1), "grp")
    residual_value = jnp.dot(
        antenna_coordinates,
        first_hot - second_hot,
        precision=highest,
        preferred_element_type=jnp.float32,
    )
    group_members = jnp.sum(group_hot, axis=1)
    vectors = (
        jnp.einsum("xb,gb->xg", residual_value, group_hot, precision=highest)
        / group_members[None, :]
    )
    owned_unique, owned_sky = (
        lax.all_to_all(unique, "chan", split_axis=2, concat_axis=1, tiled=True),
        lax.all_to_all(sky_model, "chan", split_axis=2, concat_axis=1, tiled=True),
    )
    owned_count = owned_unique.shape[2]
    owned_vectors = lax.dynamic_slice_in_dim(
        vectors, lax.axis_index("chan") * owned_count, owned_count, 1
    )
    cosines, sine_table, frequency = delay_tables(CHANNEL_COUNT, CHANNEL_COUNT, NDLY)
    cross_ratio = complex_product(owned_unique, conjugated_value(owned_sky))
    real_part, imag_part = delay_coefficients(cross_ratio, cosines, sine_table)
    phases = smooth_phase(real_part, imag_part, cosines, sine_table)
    totals = lax.psum(channel_sums(owned_unique, owned_sky, phases, owned_vectors), ("grp", "chan"))
    delay_slope = slope_fit(slope_terms(totals, frequency))
    owned_done = apply_fit(owned_unique, totals, frequency, delay_slope, owned_vectors)
    calibrated = lax.all_to_all(owned_done, "chan", split_axis=1, concat_axis=2, tiled=True)
    return (current_gain, calibrated, chi_square)


def solution(mesh):
    in_specs = (
        P(None, "chan", "grp"),
        P(None, "grp"),
        P("grp", None),
        P(None, "chan", "grp"),
        P(None, "chan", None),
        P(),
    )
    out_specs = (P(None, "chan", None), P(None, "chan", "grp"), P("chan"))
    return jax.shard_map(
        per_device, mesh=mesh, in_specs=in_specs, out_specs=out_specs, check_vma=False
    )
```

profile of v0, /device:TPU:32, one launch (start us, length us, event | category | flops | bytes accessed | tf_op | source)
XLA Modules:
  0.0 666.6 jit_solution(4750760497327303666)
XLA Ops:
  8.1 2.7 fusion.50
  10.8 1.7 fusion.53
  17.3 1.6 fusion.7
  19.3 2.3 fusion.149
  21.6 2.2 fusion.23
  23.8 2.6 fusion.129
  26.5 97.3 %all-reduce.15.cloned.1.call-done = (f32[2,96,350]{2,1,0:T(8,128)}, f32[96,350]{1,0:T(8,128)}) async-done(((f32[2,96,350]{2,1,0:T(8,128)}, f32[96,350]{1,0:T(8,128)}), (f32[2,96,350]{2,1,0:T(8,128)}, f32[96,350]{1,0:T(8,128)})) %all-reduce.15.cloned.1.call-update) | async-done | bytes 403216 | tf_op jit(solution)/shard_map/psum | solution.py:177
  125.7 1.6 fusion.21
  127.3 1.6 fusion.44
  133.2 1.6 fusion.4
  135.2 2.3 fusion.152
  137.5 1.9 fusion.19
  139.4 12.7 %fusion.134 = f32[2,96,350]{2,1,0:T(8,128)} fusion(f32[2,96,350]{2,1,0:T(8,128)S(1)} %fusion.19, s32[2048]{0:T(1024)S(1)} %bitcast.182, f32[1,96,2048]{2,1,0:T(8,128)S(1)} %get-tuple-element.87, f32[1,96,2048]{2,1,0:T(8,128)S(1)} %get-tuple-element.51), kind=kOutput, calls=%fused_computation.113 | convolution fusion | flops 1652684416 | bytes 2118656 | tf_op jit(solution)/shard_map/acb,nb->acn/dot_general | solution.py:42
  152.9 7.5 %all-to-all-start.1 = ((f32[2,96,128]{1,0,2:T(2,128)}), f32[2,96,128]{1,0,2:T(2,128)S(1)}, u32[]{:S(2)}, u32[]{:S(2)}) async-start(f32[2,96,128]{1,0,2:T(2,128)} %copy.22), calls=%async_computation.1 | async-start | bytes 262144 | tf_op jit(solution)/shard_map/all_to_all | solution.py:201
  160.5 2.3 fusion
  162.8 83.5 %all-reduce.13.cloned.1.call-done = (f32[2,96,350]{2,1,0:T(8,128)}, f32[96,350]{1,0:T(8,128)}) async-done(((f32[2,96,350]{2,1,0:T(8,128)}, f32[96,350]{1,0:T(8,128)}), (f32[2,96,350]{2,1,0:T(8,128)}, f32[96,350]{1,0:T(8,128)})) %all-reduce.13.cloned.1.call-update) | async-done | bytes 403216 | tf_op jit(solution)/shard_map/psum | solution.py:177
  248.3 1.6 fusion.17
  249.8 1.6 fusion.40
  255.7 1.6 fusion.6
  257.8 2.7 fusion.150
  260.4 1.9 fusion.15
  262.4 2.6 fusion.139
  265.9 93.2 %all-reduce.11.cloned.1.call-done = (f32[2,96,350]{2,1,0:T(8,128)}, f32[96,350]{1,0:T(8,128)}) async-done(((f32[2,96,350]{2,1,0:T(8,128)}, f32[96,350]{1,0:T(8,128)}), (f32[2,96,350]{2,1,0:T(8,128)}, f32[96,350]{1,0:T(8,128)})) %all-reduce.11.cloned.1.call-update) | async-done | bytes 403216 | tf_op jit(solution)/shard_map/psum | solution.py:177
  361.1 1.6 fusion.13
  362.6 1.6 fusion.36
  368.5 1.6 fusion.5
  370.5 2.3 fusion.151
  372.8 2.1 fusion.11
  374.9 2.6 fusion.144
  378.3 93.5 %all-reduce.9.cloned.1.call-done = (f32[2,96,350]{2,1,0:T(8,128)}, f32[96,350]{1,0:T(8,128)}) async-done(((f32[2,96,350]{2,1,0:T(8,128)}, f32[96,350]{1,0:T(8,128)}), (f32[2,96,350]{2,1,0:T(8,128)}, f32[96,350]{1,0:T(8,128)})) %all-reduce.9.cloned.1.call-update) | async-done | bytes 403216 | tf_op jit(solution)/shard_map/psum | solution.py:177
  473.7 1.6 fusion.32
  475.3 1.6 fusion.9
  479.3 2.0 fusion.171
  482.0 7.7 %all-to-all-start = ((f32[2,96,128]{1,0,2:T(2,128)}), f32[2,96,128]{1,0,2:T(2,128)S(1)}, u32[]{:S(2)}, u32[]{:S(2)}) async-start(f32[2,96,128]{1,0,2:T(2,128)} %copy.19), calls=%async_computation | async-start | bytes 262144 | tf_op jit(solution)/shard_map/all_to_all | solution.py:200
  489.7 2.9 multiply_subtract_fusion
  492.6 4.3 all-to-all-done
  497.2 3.5 fusion.220
  500.7 3.5 fusion.224
  504.3 3.5 fusion.168
  507.8 3.8 fusion.169
  511.6 3.9 fusion.222
  515.6 3.8 multiply_reduce_fusion.3
  519.9 76.5 %psum.78 = f32[7,1536]{1,0:T(8,128)S(1)} all-reduce(f32[7,1536]{1,0:T(8,128)S(1)} %stack.119), channel_id=1, replica_groups=mesh['grp'=16,'chan'=16] {'grp','chan'}, use_global_device_ids=true, to_apply=%region_16.17 | all-reduce | flops 10752 | bytes 86016 | tf_op jit(solution)/shard_map/psum | solution.py:211
  607.9 3.1 reshape.688
  611.0 3.4 all-to-all-start.2
  614.5 1.7 maximum_subtract_fusion
  616.3 37.4 %psum.79 = f32[96]{0:T(128)} all-reduce(f32[96]{0:T(128)S(1)} %fusion.189), channel_id=1, replica_groups=mesh['grp'=16,'chan'=16] {'grp'}, use_global_device_ids=true, to_apply=%region_23.24 | all-reduce | flops 96 | bytes 768 | tf_op jit(solution)/shard_map/psum | solution.py:187
  655.2 2.4 reshape.689
  (110 shorter events, 41.6 us)
Async XLA Ops:
  7.2 153.3 %copy-start = (f32[2,350]{1,0:T(2,128)S(1)}, f32[2,350]{1,0:T(2,128)}, u32[]{:S(2)}) copy-start(f32[2,350]{1,0:T(2,128)} %param.11) | copy-start | bytes 8404
  7.2 3.6 copy-start.3
  7.2 116.6 %all-reduce.15.cloned.1.call-start = ((), (), s32[]{:S(2)}) async-start(), calls=%async_computation.6 | async-start | bytes 884736 | tf_op jit(solution)/shard_map/psum | solution.py:177
  8.1 4.5 copy-start.2
  13.0 0.7 copy-start.5
  26.4 219.9 %all-reduce.13.cloned.1.call-start = ((), (), s32[]{:S(2)}) async-start(), calls=%async_computation.5 | async-start | bytes 884736 | tf_op jit(solution)/shard_map/psum | solution.py:177
  139.4 12.8 %copy-start.7 = (f32[2,96,128]{2,1,0:T(8,128)S(1)}, f32[2,96,128]{2,1,0:T(8,128)}, u32[]{:S(2)}) copy-start(f32[2,96,128]{2,1,0:T(8,128)} %param.9) | copy-start | bytes 294916
  152.9 224.7 %all-to-all-start.1 = ((f32[2,96,128]{1,0,2:T(2,128)}), f32[2,96,128]{1,0,2:T(2,128)S(1)}, u32[]{:S(2)}, u32[]{:S(2)}) async-start(f32[2,96,128]{1,0,2:T(2,128)} %copy.22), calls=%async_computation.1 | async-start | bytes 262144 | tf_op jit(solution)/shard_map/all_to_all | solution.py:201
  160.4 198.7 %all-reduce.11.cloned.1.call-start = ((), (), s32[]{:S(2)}) async-start(), calls=%async_computation.4 | async-start | bytes 884736 | tf_op jit(solution)/shard_map/psum | solution.py:177
  265.0 206.8 %all-reduce.9.cloned.1.call-start = ((), (), s32[]{:S(2)}) async-start(), calls=%async_computation.3 | async-start | bytes 884736 | tf_op jit(solution)/shard_map/psum | solution.py:177
  473.7 3.2 copy-start.4
  482.0 14.9 %all-to-all-start = ((f32[2,96,128]{1,0,2:T(2,128)}), f32[2,96,128]{1,0,2:T(2,128)S(1)}, u32[]{:S(2)}, u32[]{:S(2)}) async-start(f32[2,96,128]{1,0,2:T(2,128)} %copy.19), calls=%async_computation | async-start | bytes 262144 | tf_op jit(solution)/shard_map/all_to_all | solution.py:200
  489.7 7.2 %copy-start.6 = (f32[2,96,128]{1,2,0:T(8,128)S(1)}, f32[2,96,128]{1,2,0:T(8,128)}, u32[]{:S(2)}) copy-start(f32[2,96,128]{1,2,0:T(8,128)} %copy.36) | copy-start | bytes 294916
  611.0 42.7 %all-to-all-start.2 = ((f32[16,1,1536]{2,1,0:T(1,128)}), f32[16,1,1536]{2,1,0:T(1,128)S(1)}, u32[]{:S(2)}, u32[]{:S(2)}) async-start(f32[16,1,1536]{2,1,0:T(1,128)} %reshape.688), calls=%async_computation.2 | async-start | bytes 196608 | tf_op jit(solution)/shard_map/all_to_all | solution.py:214
  654.3 5.3 copy-start.1
Sparse Core Ops, SparseCore 0:
  26.5 97.1 all-reduce.14
  152.3 93.9 all-reduce.12
  265.1 93.9 all-reduce.10
  377.7 94.0 all-reduce.8
where the time goes:
time: 676 us; the launch traced here: 667 us
  waiting for transfers between devices  372 us (55%)
  blocking collectives  114 us (17%)
  matrix products  100 us (15%)
  other arithmetic  25.6 us (4%)
  between operations  23 us (3%)
  starting transfers between devices  18.8 us (3%)
  local copies, waits for them, and re-layouts  13.3 us (2%)
    psum x4, waiting for transfers between devices, per_device(): lax.psum((update_numerator, update_denominator), 'grp')  368 us
    psum x1, blocking collectives, per_device(): lax.psum(channel_sums(owned_unique, owned_sky, phases, owned_vectors), ('...  76.5 us
    psum x1, blocking collectives, per_device(): chi_square = lax.psum(jnp.sum(absolute_size(misfit), axis=1), 'grp')  37.4 us
    dot_general x13, matrix products, collect(): return jnp.einsum('acb,nb->acn', source, lookup, precision=highest)  33.5 us
    dot_general x15, matrix products, spread(): return jnp.einsum('acn,nb->acb', source, lookup, precision=highest)  22 us
    dot_general x13, matrix products, collect_real(): return jnp.einsum('cb,nb->cn', source, lookup, precision=highest)  19.8 us
  transfers between devices with their start and end apart: 7, of which 5 were waited for; matrix products, arithmetic and copies ran while one was open for 7% of the time, Pallas kernels for 0%

commit v1 on v0

v1 whole, which is shorter than its diff:
```python
import functools

import jax
import jax.numpy as jnp
import numpy as np
from jax import lax
from jax.experimental import pallas as pl
from jax.experimental.pallas import tpu as pltpu
from jax.sharding import PartitionSpec as P

CHANNEL_COUNT = 1536
NDLY = 64
ITERS = 4
RIDGE = 0.5
EPSILON = 1e-06

N = 16
ANT = 350
ANT_PAD = 384
CH = 96
BL = 2048
GRP = 128
TILE = 256
STEPS = BL // TILE
ROWS = 8
OWNERS = CH // ROWS

MESH = pl.DeviceIdType.MESH
HIGHEST = lax.Precision.HIGHEST
f32 = jnp.float32
bf16 = jnp.bfloat16


def owner_of(block):
    return block + 1 + block // 4


def two_parts(number):
    first = number.astype(bf16)
    return first, (number - first.astype(f32)).astype(bf16)


def dot(left, right):
    return jnp.dot(left, right, preferred_element_type=f32)


def dot_last(left, right):
    return lax.dot_general(left, right, (((1,), (1,)), ((), ())), preferred_element_type=f32)


def solve_pair(entry_xx, entry_xy, entry_yy, right_x, right_y):
    ridge_shift = 0.001 * (entry_xx + entry_yy) + EPSILON
    diag_first = entry_xx + ridge_shift
    diag_second = entry_yy + ridge_shift
    determinant = diag_first * diag_second - entry_xy * entry_xy
    return (
        (diag_second * right_x - entry_xy * right_y) / determinant,
        (diag_first * right_y - entry_xy * right_x) / determinant,
    )


def delay_tables():
    channel_ids = np.arange(CHANNEL_COUNT)
    turns = (channel_ids[:, None] * (np.arange(NDLY)[None, :] - NDLY // 2)) % CHANNEL_COUNT
    angles = 2.0 * np.pi / CHANNEL_COUNT * turns
    cosines = np.cos(angles).reshape(N, CH, NDLY)
    sines = np.sin(angles).reshape(N, CH, NDLY)
    cos_t = cosines.transpose(0, 2, 1) / CHANNEL_COUNT
    sin_t = sines.transpose(0, 2, 1) / CHANNEL_COUNT
    ahead = np.concatenate(
        [np.concatenate([cos_t, sin_t], axis=2), np.concatenate([-sin_t, cos_t], axis=2)], axis=1
    )
    back = np.concatenate([sines, cosines], axis=2)
    return ahead.astype(np.float32), back.astype(np.float32)


def kernel(
    vis, ants, gid, sky, start, coords, ahead_hbm, back_hbm,
    gains_out, cal_out, chi_out,
    hot_spread, hot_collect, grp_spread, grp_collect, pair, gain, gain2, acc_grp, unique, unique2,
    acc_ant, rs_buf, ahead, back, ratio, part, coef, coef_buf, square_buf, tot_buf, slope_buf, chi_acc,
    vec_acc, table_sem, rs_send, rs_recv, ag_send, ag_recv, cr_send, cr_recv, ca_send, ca_recv,
    tot_send, tot_recv, slope_send, slope_recv,
):
    me = lax.axis_index("grp")
    band = lax.axis_index("chan")

    def on_grp(other):
        return (other, band)

    def on_chan(other):
        return (me, other)

    def others(body):
        def step(r, carry):
            body(r)
            return carry

        lax.fori_loop(1, N, step, 0)

    barrier = pltpu.get_barrier_semaphore()

    def greet(r):
        pl.semaphore_signal(barrier, inc=1, device_id=on_grp(lax.rem(me + r, N)), device_id_type=MESH)
        pl.semaphore_signal(barrier, inc=1, device_id=on_chan(lax.rem(band + r, N)), device_id_type=MESH)

    others(greet)

    copy_ahead = pltpu.make_async_copy(ahead_hbm.at[band], ahead, table_sem.at[0])
    copy_back = pltpu.make_async_copy(back_hbm.at[band], back, table_sem.at[1])
    copy_ahead.start()
    copy_back.start()

    vec_acc[...] = jnp.zeros_like(vec_acc)
    coords_1, coords_rest = two_parts(coords[...])
    coords_2 = coords_rest

    def build(t, carry):
        cols = pl.ds(pl.multiple_of(t * TILE, TILE), TILE)
        ant_ids = lax.broadcasted_iota(jnp.int32, (ANT_PAD, TILE), 0)
        grp_ids = lax.broadcasted_iota(jnp.int32, (GRP, TILE), 0)
        one = jnp.ones((), f32)
        nil = jnp.zeros((), f32)
        p_hot = jnp.where(ant_ids == ants[0:1, cols], one, nil).astype(bf16)
        q_hot = jnp.where(ant_ids == ants[1:2, cols], one, nil).astype(bf16)
        g_hot = jnp.where(grp_ids == gid[0:1, cols], one, nil).astype(bf16)
        for half in range(2):
            hot_spread[t, half * ANT_PAD:(half + 1) * ANT_PAD, :TILE] = p_hot
            hot_spread[t, half * ANT_PAD:(half + 1) * ANT_PAD, TILE:] = q_hot
            hot_collect[t, :, half * TILE:(half + 1) * TILE] = p_hot
            hot_collect[t, :, (2 + half) * TILE:(3 + half) * TILE] = q_hot
            grp_spread[t, half * GRP:(half + 1) * GRP, :] = g_hot
            grp_collect[t, :, half * TILE:(half + 1) * TILE] = g_hot
        diff = p_hot - q_hot
        place = dot(coords_1, diff) + dot(coords_2, diff)
        row = lax.broadcasted_iota(jnp.int32, place.shape, 0)
        place = jnp.where(row == 2, 1.0, place)
        place_1, place_2 = two_parts(place)
        vec_acc[...] += dot_last(jnp.concatenate([place_1, place_2], axis=1),
                                 jnp.concatenate([g_hot, g_hot], axis=1))
        return carry

    lax.fori_loop(0, STEPS, build, 0)

    gain[:, :, ANT_PAD - 128:] = jnp.zeros((2, CH, 128), f32)
    gain[:, :, :ANT] = start[...]

    def group_fit():
        g = gain[...].reshape(2 * CH, ANT_PAD)
        g_1, g_2 = two_parts(g)
        gain2[:, :ANT_PAD] = g_1
        gain2[:, ANT_PAD:] = g_2
        acc_grp[...] = jnp.zeros_like(acc_grp)

        def step(t, carry):
            cols = pl.ds(pl.multiple_of(t * TILE, TILE), TILE)
            pq = dot(gain2[...], hot_spread[t])
            pair[t] = pq
            a, b = pq[:CH, :TILE], pq[CH:, :TILE]
            c, d = pq[:CH, TILE:], pq[CH:, TILE:]
            x, y = vis[0, :, cols], vis[1, :, cols]
            wr = a * c + b * d
            wi = b * c - a * d
            rows = jnp.concatenate([x * wr + y * wi, y * wr - x * wi, wr * wr + wi * wi], axis=0)
            r_1, r_2 = two_parts(rows)
            acc_grp[...] += dot_last(jnp.concatenate([r_1, r_2], axis=1), grp_collect[t])
            return carry

        lax.fori_loop(0, STEPS, step, 0)
        scale = 1.0 / (acc_grp[2 * CH:, :] + RIDGE)
        u = jnp.concatenate([acc_grp[:CH, :] * scale, acc_grp[CH:2 * CH, :] * scale], axis=0)
        unique[...] = u
        u_1, u_2 = two_parts(u)
        unique2[:, :GRP] = u_1
        unique2[:, GRP:] = u_2

    def antenna_sums():
        acc_ant[...] = jnp.zeros_like(acc_ant)

        def step(t, carry):
            cols = pl.ds(pl.multiple_of(t * TILE, TILE), TILE)
            uu = dot(unique2[...], grp_spread[t])
            s, v = uu[:CH], uu[CH:]
            pq = pair[t]
            a, b = pq[:CH, :TILE], pq[CH:, :TILE]
            c, d = pq[:CH, TILE:], pq[CH:, TILE:]
            x, y = vis[0, :, cols], vis[1, :, cols]
            zr = s * x + v * y
            zi = s * y - v * x
            size = s * s + v * v
            for_p = jnp.concatenate([c * zr - d * zi, c * zi + d * zr, size * (c * c + d * d)], axis=0)
            for_q = jnp.concatenate([a * zr + b * zi, b * zr - a * zi, size * (a * a + b * b)], axis=0)
            p_1, p_2 = two_parts(for_p)
            q_1, q_2 = two_parts(for_q)
            sums = dot_last(jnp.concatenate([p_1, p_2, q_1, q_2], axis=1), hot_collect[t])
            acc_ant[...] += sums.reshape(3, CH, ANT_PAD)
            return carry

        lax.fori_loop(0, STEPS, step, 0)

    def rs_copy(block):
        rows = pl.ds(pl.multiple_of(block * ROWS, ROWS), ROWS)
        return pltpu.make_async_remote_copy(
            src_ref=acc_ant.at[:, rows, :], dst_ref=rs_buf.at[me],
            send_sem=rs_send.at[block], recv_sem=rs_recv.at[me],
            device_id=on_grp(owner_of(block)), device_id_type=MESH)

    def rs_arrival(source):
        return pltpu.make_async_remote_copy(
            src_ref=rs_buf.at[source], dst_ref=rs_buf.at[source],
            send_sem=rs_send.at[0], recv_sem=rs_recv.at[source],
            device_id=on_grp(source), device_id_type=MESH)

    def ag_copy(block, other):
        rows = pl.ds(pl.multiple_of(block * ROWS, ROWS), ROWS)
        return pltpu.make_async_remote_copy(
            src_ref=gain.at[:, rows, :], dst_ref=gain.at[:, rows, :],
            send_sem=ag_send.at[other], recv_sem=ag_recv.at[block],
            device_id=on_grp(other), device_id_type=MESH)

    def blocks(body):
        def step(k, carry):
            block = lax.rem(me + k, OWNERS)

            @pl.when(owner_of(block) != me)
            def _():
                body(block)

            return carry

        lax.fori_loop(0, OWNERS, step, 0)

    def update_gains():
        blocks(lambda block: rs_copy(block).start())

        def mine(block, carry):
            @pl.when(owner_of(block) == me)
            def _():
                rows = pl.ds(pl.multiple_of(block * ROWS, ROWS), ROWS)
                rs_buf[me] = acc_ant[:, rows, :]
                others(lambda r: rs_arrival(lax.rem(me + r, N)).wait_recv())
                total = rs_buf[0]
                for source in range(1, N):
                    total = total + rs_buf[source]
                share = 0.5 / (total[2] + RIDGE)
                gain[0, rows, :] = 0.5 * gain[0, rows, :] + total[0] * share
                gain[1, rows, :] = 0.5 * gain[1, rows, :] + total[1] * share
                others(lambda r: ag_copy(block, lax.rem(me + r, N)).start())
                others(lambda r: ag_copy(block, lax.rem(me + r, N)).wait_send())

            return carry

        lax.fori_loop(0, OWNERS, mine, 0)
        blocks(lambda block: rs_copy(block).wait_send())
        blocks(lambda block: ag_copy(block, owner_of(block)).wait_recv())

    def iteration(index, carry):
        group_fit()
        antenna_sums()

        @pl.when(index == 0)
        def _():
            pl.semaphore_wait(barrier, 2 * (N - 1))

        update_gains()
        return carry

    lax.fori_loop(0, ITERS, iteration, 0)
    group_fit()
    gains_out[...] = gain[:, :, :ANT]

    ur, ui = unique[:CH, :], unique[CH:, :]
    sr, si = sky[0], sky[1]
    ratio[:CH, :] = ur * sr + ui * si
    ratio[CH:, :] = ui * sr - ur * si
    copy_ahead.wait()
    part[...] = jnp.dot(ahead[...], ratio[...], precision=HIGHEST, preferred_element_type=f32)

    def cr_copy(other):
        rows = pl.ds(pl.multiple_of(other * 8, 8), 8)
        return pltpu.make_async_remote_copy(
            src_ref=part.at[rows, :], dst_ref=coef_buf.at[band],
            send_sem=cr_send.at[other], recv_sem=cr_recv.at[band],
            device_id=on_chan(other), device_id_type=MESH)

    def cr_arrival(source):
        return pltpu.make_async_remote_copy(
            src_ref=coef_buf.at[source], dst_ref=coef_buf.at[source],
            send_sem=cr_send.at[0], recv_sem=cr_recv.at[source],
            device_id=on_chan(source), device_id_type=MESH)

    def ca_copy(source, other):
        rows = pl.ds(pl.multiple_of(source * 8, 8), 8)
        return pltpu.make_async_remote_copy(
            src_ref=coef.at[rows, :], dst_ref=coef.at[rows, :],
            send_sem=ca_send.at[other], recv_sem=ca_recv.at[source],
            device_id=on_chan(other), device_id_type=MESH)

    others(lambda r: cr_copy(lax.rem(band + r, N)).start())
    my_rows = pl.ds(pl.multiple_of(band * 8, 8), 8)
    coef_buf[band] = part[my_rows, :]
    others(lambda r: cr_arrival(lax.rem(band + r, N)).wait_recv())
    others(lambda r: cr_copy(lax.rem(band + r, N)).wait_send())
    total_coef = coef_buf[0]
    for source in range(1, N):
        total_coef = total_coef + coef_buf[source]
    coef[my_rows, :] = total_coef
    others(lambda r: ca_copy(band, lax.rem(band + r, N)).start())

    chi_acc[...] = jnp.zeros_like(chi_acc)

    def misfit(t, carry):
        cols = pl.ds(pl.multiple_of(t * TILE, TILE), TILE)
        uu = dot(unique2[...], grp_spread[t])
        s, v = uu[:CH], uu[CH:]
        pq = pair[t]
        a, b = pq[:CH, :TILE], pq[CH:, :TILE]
        c, d = pq[:CH, TILE:], pq[CH:, TILE:]
        wr = a * c + b * d
        wi = b * c - a * d
        er = vis[0, :, cols] - (wr * s - wi * v)
        ei = vis[1, :, cols] - (wr * v + wi * s)
        e = er * er + ei * ei
        chi_acc[...] += e[:, :128] + e[:, 128:]
        return carry

    lax.fori_loop(0, STEPS, misfit, 0)

    east = vec_acc[0:1, :] / vec_acc[2:3, :]
    north = vec_acc[1:2, :] / vec_acc[2:3, :]
    model = sr * sr + si * si
    squared = model * model
    copy_back.wait()
    others(lambda r: ca_copy(lax.rem(band + r, N), band).wait_recv())
    others(lambda r: ca_copy(band, lax.rem(band + r, N)).wait_send())
    phases = jnp.dot(back[...], coef[...], precision=HIGHEST, preferred_element_type=f32)

    weighted = model * phases
    fields = [
        ur * ur + ui * ui, model, squared * (east * east), squared * (east * north),
        squared * (north * north), weighted * east, weighted * north, chi_acc[...],
    ]
    lane = lax.broadcasted_iota(jnp.int32, (CH, 128), 1)
    table = jnp.zeros((CH, 128), f32)
    for place, field in enumerate(fields):
        table = jnp.where(lane == place, jnp.sum(field, axis=1, keepdims=True), table)
    square_buf[CH:, :] = jnp.zeros((128 - CH, 128), f32)
    square_buf[:CH, :] = table
    tot_buf[me] = square_buf[...].T[:8, :]

    def tot_copy(source, other):
        return pltpu.make_async_remote_copy(
            src_ref=tot_buf.at[source], dst_ref=tot_buf.at[source],
            send_sem=tot_send.at[other], recv_sem=tot_recv.at[source],
            device_id=on_grp(other), device_id_type=MESH)

    others(lambda r: tot_copy(me, lax.rem(me + r, N)).start())
    others(lambda r: tot_copy(lax.rem(me + r, N), me).wait_recv())
    others(lambda r: tot_copy(me, lax.rem(me + r, N)).wait_send())
    totals = tot_buf[0]
    for source in range(1, N):
        totals = totals + tot_buf[source]
    chi_out[...] = totals[7:8, :CH]

    channel = band * CH + lax.broadcasted_iota(jnp.int32, (1, 128), 1)
    frequency = 1.0 + channel.astype(f32) * (1.0 / CHANNEL_COUNT)
    squares = frequency * frequency
    slope_buf[band] = jnp.concatenate(
        [squares * totals[2:3], squares * totals[3:4], squares * totals[4:5],
         frequency * totals[5:6], frequency * totals[6:7], jnp.zeros((3, 128), f32)], axis=0)

    def slope_copy(source, other):
        return pltpu.make_async_remote_copy(
            src_ref=slope_buf.at[source], dst_ref=slope_buf.at[source],
            send_sem=slope_send.at[other], recv_sem=slope_recv.at[source],
            device_id=on_chan(other), device_id_type=MESH)

    others(lambda r: slope_copy(band, lax.rem(band + r, N)).start())
    tilt_east, tilt_north = solve_pair(
        totals[2:3], totals[3:4], totals[4:5], totals[5:6], totals[6:7])
    amplitude = jnp.sqrt((totals[0:1] + EPSILON) / (totals[1:2] + EPSILON))
    scale = 1.0 / amplitude
    others(lambda r: slope_copy(lax.rem(band + r, N), band).wait_recv())
    others(lambda r: slope_copy(band, lax.rem(band + r, N)).wait_send())
    slopes = slope_buf[0]
    for source in range(1, N):
        slopes = slopes + slope_buf[source]
    terms = jnp.sum(slopes, axis=1, keepdims=True)
    slope_east, slope_north = solve_pair(
        terms[0:1], terms[1:2], terms[2:3], terms[3:4], terms[4:5])
    tilt_east = tilt_east - frequency * slope_east
    tilt_north = tilt_north - frequency * slope_north
    square_buf[0:8, :] = jnp.concatenate(
        [frequency, tilt_east, tilt_north, scale, jnp.zeros((4, 128), f32)], axis=0)
    columns = square_buf[...].T[:CH, :]
    along = slope_east * east + slope_north * north
    turn = columns[:, 0:1] * along + columns[:, 1:2] * east + columns[:, 2:3] * north
    rotation_cos = jnp.cos(turn) * columns[:, 3:4]
    rotation_sin = jnp.sin(turn) * columns[:, 3:4]
    cal_out[0] = ur * rotation_cos + ui * rotation_sin
    cal_out[1] = ui * rotation_cos - ur * rotation_sin


def per_device(ahead, back, vis, ants, gid, sky, start, coords):
    coords = jnp.pad(coords, ((0, 6), (0, ANT_PAD - ANT)))
    vmem = pl.BlockSpec(memory_space=pltpu.VMEM)
    dma = pltpu.SemaphoreType.DMA
    gains, cal, chi = pl.pallas_call(
        kernel,
        out_shape=(
            jax.ShapeDtypeStruct((2, CH, ANT), f32),
            jax.ShapeDtypeStruct((2, CH, GRP), f32),
            jax.ShapeDtypeStruct((1, CH), f32),
        ),
        in_specs=[vmem] * 6 + [pl.BlockSpec(memory_space=pl.ANY)] * 2,
        out_specs=(vmem, vmem, vmem),
        scratch_shapes=[
            pltpu.VMEM((STEPS, 2 * ANT_PAD, 2 * TILE), bf16),
            pltpu.VMEM((STEPS, ANT_PAD, 4 * TILE), bf16),
            pltpu.VMEM((STEPS, 2 * GRP, TILE), bf16),
            pltpu.VMEM((STEPS, GRP, 2 * TILE), bf16),
            pltpu.VMEM((STEPS, 2 * CH, 2 * TILE), f32),
            pltpu.VMEM((2, CH, ANT_PAD), f32),
            pltpu.VMEM((2 * CH, 2 * ANT_PAD), bf16),
            pltpu.VMEM((3 * CH, GRP), f32),
            pltpu.VMEM((2 * CH, GRP), f32),
            pltpu.VMEM((2 * CH, 2 * GRP), bf16),
            pltpu.VMEM((3, CH, ANT_PAD), f32),
            pltpu.VMEM((N, 3, ROWS, ANT_PAD), f32),
            pltpu.VMEM((2 * NDLY, 2 * CH), f32),
            pltpu.VMEM((CH, 2 * NDLY), f32),
            pltpu.VMEM((2 * CH, GRP), f32),
            pltpu.VMEM((2 * NDLY, GRP), f32),
            pltpu.VMEM((2 * NDLY, GRP), f32),
            pltpu.VMEM((N, 8, GRP), f32),
            pltpu.VMEM((128, 128), f32),
            pltpu.VMEM((N, 8, 128), f32),
            pltpu.VMEM((N, 8, 128), f32),
            pltpu.VMEM((CH, 128), f32),
            pltpu.VMEM((8, GRP), f32),
            dma((2,)),
        ] + [dma((N,))] * 12,
        compiler_params=pltpu.CompilerParams(
            collective_id=0, has_side_effects=True, vmem_limit_bytes=48 * 1024 * 1024),
        cost_estimate=pl.CostEstimate(flops=20_000_000_000, bytes_accessed=4_000_000, transcendentals=0),
    )(vis, ants, gid, sky, start, coords, ahead, back)
    return gains, cal, chi.reshape(CH)


def solution(mesh):
    ahead, back = delay_tables()

    def program(vis, ants, gid, sky, start, coords):
        return jax.shard_map(
            functools.partial(per_device, ahead, back),
            mesh=mesh,
            in_specs=(
                P(None, "chan", "grp"),
                P(None, "grp"),
                P("grp", None),
                P(None, "chan", "grp"),
                P(None, "chan", None),
                P(),
            ),
            out_specs=(P(None, "chan", None), P(None, "chan", "grp"), P("chan")),
            check_vma=False,
        )(vis, ants, gid, sky, start, coords)

    return program
```

time: 676 us -> 150 us (0.22)
  the two profiles are of different devices: /device:TPU:32 before, /device:TPU:1 now
where the time goes in v1:
time: 150 us; the launch traced here: 149 us
  Pallas kernels  139 us (93%)
  local copies, waits for them, and re-layouts  9.96 us (7%)
    pallas_call x1, Pallas kernels, per_device(): pl.pallas_call(kernel, out_shape=(jax.ShapeDtypeStruct((2, CH, ANT), f32)...  139 us
    unnamed x17, local copies, waits for them, and re-layouts  9.26 us

profile of v1, /device:TPU:1, one launch (start us, length us, event | category | flops | bytes accessed | tf_op | source)
XLA Modules:
  0.0 149.2 jit_solution(10306437782547210424)
XLA Ops:
  0.6 0.7 pad.4.coords
  1.3 0.0 copy-start
  1.3 1.4 copy-done
  2.7 0.0 copy-start.1
  2.7 1.0 copy-done.1
  3.7 0.0 copy-start.2
  3.7 0.9 copy-done.2
  4.6 0.0 copy-start.3
  4.6 0.7 copy-done.3
  5.3 0.0 copy-start.4
  5.3 0.7 copy-done.4
  6.0 0.0 copy-start.5
  6.0 1.6 %copy-done.5 = f32[16,128,192]{2,1,0:T(8,128)S(1)} copy-done((f32[16,128,192]{2,1,0:T(8,128)S(1)}, f32[16,128,192]{2,1,0:T(8,128)}, u32[]{:S(2)}) %copy-start.5) | copy-done | bytes 1572888
  7.6 0.0 copy-start.6
  7.6 1.1 copy-done.6
  8.7 138.6 %shard_map.103 = (f32[2,96,350]{2,1,0:T(8,128)S(1)}, f32[2,96,128]{2,1,0:T(8,128)S(1)}, f32[1,96]{1,0:T(1,128)S(1)}) custom-call(f32[2,96,2048]{2,1,0:T(8,128)S(1)} %copy-done, s32[2,2048]{1,0:T(2,128)S(1)} %copy-done.3, s32[1,2048]{1,0:T(1,128)S(1)} %copy-done.4, f32[2,96,128]{2,1,0:T(8,128)S(1)} %copy-done.2, f32[2,96,350]{2,1,0:T(8,128)S(1)} %copy-done.1, ...), custom_call_target="tpu_custom_call" | custom-call | flops 20000000000 | bytes 4000000 | tf_op jit(solution)/shard_map/pallas_call | solution.py:408
  147.3 0.7 copy.14
  148.1 0.6 copy.15
  148.7 0.5 copy.16
Async XLA Ops:
  1.3 1.4 copy-start
  2.7 1.0 copy-start.1
  3.7 0.9 copy-start.2
  4.6 0.7 copy-start.3
  5.3 0.7 copy-start.4
  6.0 1.6 %copy-start.5 = (f32[16,128,192]{2,1,0:T(8,128)S(1)}, f32[16,128,192]{2,1,0:T(8,128)}, u32[]{:S(2)}) copy-start(f32[16,128,192]{2,1,0:T(8,128)} %constant.7.clone.ahead_hbm) | copy-start | bytes 4718596
  7.6 1.1 copy-start.6

commit v2 on v1

v2 whole, which is shorter than its diff:
```python
import functools

import jax
import jax.numpy as jnp
import numpy as np
from jax import lax
from jax.experimental import pallas as pl
from jax.experimental.pallas import tpu as pltpu
from jax.sharding import PartitionSpec as P

CHANNEL_COUNT = 1536
NDLY = 64
ITERS = 4
RIDGE = 0.5
EPSILON = 1e-06

N = 16
ANT = 350
ANT_PAD = 384
CH = 96
CHUNKS = 3
CHK = CH // CHUNKS
BL = 2048
GRP = 128
TILE = 256
STEPS = BL // TILE
OWN = GRP // N
LANES = 128
UNITS = (CHK // 8) * (ANT_PAD // LANES)

MESH = pl.DeviceIdType.MESH
HIGHEST = lax.Precision.HIGHEST
f32 = jnp.float32
bf16 = jnp.bfloat16


def owner_of(unit):
    return unit + 1 + unit // 4


def two_parts(number):
    first = number.astype(bf16)
    rest = (number - first.astype(f32)).astype(bf16)
    return jnp.concatenate([first, rest], axis=0)


def joined(parts):
    half = parts.shape[0] // 2
    return parts[:half] + parts[half:]


def dot(left, right):
    return jnp.dot(left, right, preferred_element_type=f32)


def dot_last(left, right):
    return lax.dot_general(left, right, (((1,), (1,)), ((), ())), preferred_element_type=f32)


def exact_dot(left, right):
    return jnp.dot(left, right, precision=HIGHEST, preferred_element_type=f32)


def solve_pair(entry_xx, entry_xy, entry_yy, right_x, right_y):
    ridge_shift = 0.001 * (entry_xx + entry_yy) + EPSILON
    diag_first = entry_xx + ridge_shift
    diag_second = entry_yy + ridge_shift
    determinant = diag_first * diag_second - entry_xy * entry_xy
    return (
        (diag_second * right_x - entry_xy * right_y) / determinant,
        (diag_first * right_y - entry_xy * right_x) / determinant,
    )


def delay_tables():
    channel_ids = np.arange(CHANNEL_COUNT)
    turns = (channel_ids[:, None] * (np.arange(NDLY)[None, :] - NDLY // 2)) % CHANNEL_COUNT
    angles = 2.0 * np.pi / CHANNEL_COUNT * turns
    cosines = np.cos(angles).reshape(N, CH, NDLY).transpose(0, 2, 1)
    sines = np.sin(angles).reshape(N, CH, NDLY).transpose(0, 2, 1)
    ahead = np.concatenate(
        [np.concatenate([cosines, sines], axis=2), np.concatenate([-sines, cosines], axis=2)], axis=1
    )
    back = np.zeros((2 * NDLY, N, LANES))
    back[:NDLY, :, :CH] = sines.transpose(1, 0, 2)
    back[NDLY:, :, :CH] = cosines.transpose(1, 0, 2)
    return (ahead / CHANNEL_COUNT).astype(np.float32), back.reshape(2 * NDLY, N * LANES).astype(np.float32)


def kernel(
    vis_hbm, ants_hbm, gid_hbm, sky_hbm, start_hbm, coords_hbm, ahead_hbm, back_hbm,
    gains_out, cal_out, chi_out,
    vis, ants, gid, sky, start, coords, ahead, back,
    hot, grp_hot, pair, gain, gain2, acc_grp, unique, unique2, acc_sum, acc_ant, rs_buf,
    ratio, part, coef_buf, model_t, model_band, square, vec_acc, vec_t, chi_acc,
    band_send_buf, band_buf, tot_buf,
    load_sem, rs_send, rs_recv, ag_send, ag_recv, mod_send, mod_recv, cr_send, cr_recv,
    band_send, band_recv, tot_send, tot_recv,
):
    me = lax.axis_index("grp")
    band = lax.axis_index("chan")
    i_own = lax.rem(me, 5) != 0
    my_unit = me - 1 - me // 5

    def others(body):
        for r in range(1, N):
            body(r)

    def grp_other(r):
        return lax.rem(me + r, N)

    def chan_other(r):
        return lax.rem(band + r, N)

    loads = [
        pltpu.make_async_copy(ants_hbm, ants, load_sem.at[0]),
        pltpu.make_async_copy(gid_hbm, gid, load_sem.at[1]),
        pltpu.make_async_copy(coords_hbm, coords, load_sem.at[2]),
        pltpu.make_async_copy(start_hbm, start, load_sem.at[3]),
        pltpu.make_async_copy(vis_hbm, vis, load_sem.at[4]),
        pltpu.make_async_copy(sky_hbm, sky, load_sem.at[5]),
        pltpu.make_async_copy(ahead_hbm.at[band], ahead, load_sem.at[6]),
        pltpu.make_async_copy(back_hbm, back, load_sem.at[7]),
    ]
    for load in loads:
        load.start()

    barrier = pltpu.get_barrier_semaphore()

    def greet(r):
        pl.semaphore_signal(barrier, inc=1, device_id=(grp_other(r), band), device_id_type=MESH)
        pl.semaphore_signal(barrier, inc=1, device_id=(me, chan_other(r)), device_id_type=MESH)

    others(greet)

    loads[0].wait()
    loads[1].wait()
    loads[2].wait()
    vec_acc[...] = jnp.zeros_like(vec_acc)
    gain[:, :, ANT_PAD - LANES:] = jnp.zeros((2, CH, LANES), f32)
    gain[0, :8, :] = jnp.zeros((8, ANT_PAD), f32)
    gain[0, 0:2, :ANT] = coords[...]
    places = two_parts(gain[0, :8, :])

    def build(t, carry):
        cols = pl.ds(pl.multiple_of(t * TILE, TILE), TILE)
        ant_ids = lax.broadcasted_iota(jnp.int32, (ANT_PAD, TILE), 0)
        grp_ids = lax.broadcasted_iota(jnp.int32, (GRP, TILE), 0)
        p_hot = jnp.where(ant_ids == ants[0:1, cols], 1.0, 0.0).astype(bf16)
        q_hot = jnp.where(ant_ids == ants[1:2, cols], 1.0, 0.0).astype(bf16)
        g_hot = jnp.where(grp_ids == gid[0:1, cols], 1.0, 0.0).astype(bf16)
        hot[t, :, :TILE] = p_hot
        hot[t, :, TILE:] = q_hot
        grp_hot[t] = g_hot
        place = joined(dot(places, p_hot - q_hot))
        row = lax.broadcasted_iota(jnp.int32, place.shape, 0)
        place = jnp.where(row == 2, 1.0, place)
        vec_acc[...] += joined(dot_last(two_parts(place), g_hot))
        return carry

    lax.fori_loop(0, STEPS, build, 0)

    loads[3].wait()
    gain[:, :, :ANT] = start[...]
    loads[4].wait()

    def rows_of(chunk):
        return pl.ds(pl.multiple_of(chunk * CHK, CHK), CHK)

    def group_fit(chunk):
        mine = rows_of(chunk)
        gain2[...] = two_parts(gain[:, mine, :].reshape(2 * CHK, ANT_PAD))
        acc_grp[...] = jnp.zeros_like(acc_grp)

        def step(t, carry):
            cols = pl.ds(pl.multiple_of(t * TILE, TILE), TILE)
            pq = joined(dot(gain2[...], hot[t]))
            pair[t] = pq
            a, b = pq[:CHK, :TILE], pq[CHK:, :TILE]
            c, d = pq[:CHK, TILE:], pq[CHK:, TILE:]
            x, y = vis[0, mine, cols], vis[1, mine, cols]
            wr = a * c + b * d
            wi = b * c - a * d
            rows = jnp.concatenate([x * wr + y * wi, y * wr - x * wi, wr * wr + wi * wi], axis=0)
            acc_grp[...] += dot_last(two_parts(rows), grp_hot[t])
            return carry

        lax.fori_loop(0, STEPS, step, 0, unroll=8)
        sums = joined(acc_grp[...])
        scale = 1.0 / (sums[2 * CHK:] + RIDGE)
        ur, ui = sums[:CHK] * scale, sums[CHK:2 * CHK] * scale
        unique[0, mine, :] = ur
        unique[1, mine, :] = ui
        unique2[...] = two_parts(jnp.concatenate([ur, ui], axis=0))

    def antenna_sums(chunk):
        mine = rows_of(chunk)
        acc_sum[...] = jnp.zeros_like(acc_sum)

        def step(t, carry):
            cols = pl.ds(pl.multiple_of(t * TILE, TILE), TILE)
            uu = joined(dot(unique2[...], grp_hot[t]))
            s, v = uu[:CHK], uu[CHK:]
            pq = pair[t]
            a, b = pq[:CHK, :TILE], pq[CHK:, :TILE]
            c, d = pq[:CHK, TILE:], pq[CHK:, TILE:]
            x, y = vis[0, mine, cols], vis[1, mine, cols]
            zr = s * x + v * y
            zi = s * y - v * x
            size = s * s + v * v
            for_p = jnp.concatenate([c * zr - d * zi, c * zi + d * zr, size * (c * c + d * d)], axis=0)
            for_q = jnp.concatenate([a * zr + b * zi, b * zr - a * zi, size * (a * a + b * b)], axis=0)
            acc_sum[...] += dot_last(two_parts(jnp.concatenate([for_p, for_q], axis=1)), hot[t])
            return carry

        lax.fori_loop(0, STEPS, step, 0, unroll=8)
        acc_ant[chunk] = joined(acc_sum[...]).reshape(3, CHK, ANT_PAD)

    def misfit(chunk):
        mine = rows_of(chunk)
        chi_acc[mine, :] = jnp.zeros((CHK, LANES), f32)

        def step(t, carry):
            cols = pl.ds(pl.multiple_of(t * TILE, TILE), TILE)
            uu = joined(dot(unique2[...], grp_hot[t]))
            s, v = uu[:CHK], uu[CHK:]
            pq = pair[t]
            a, b = pq[:CHK, :TILE], pq[CHK:, :TILE]
            c, d = pq[:CHK, TILE:], pq[CHK:, TILE:]
            wr = a * c + b * d
            wi = b * c - a * d
            er = vis[0, mine, cols] - (wr * s - wi * v)
            ei = vis[1, mine, cols] - (wr * v + wi * s)
            e = er * er + ei * ei
            chi_acc[mine, :] += e[:, :LANES] + e[:, LANES:]
            return carry

        lax.fori_loop(0, STEPS, step, 0, unroll=8)

    def place_of(unit):
        across = ANT_PAD // LANES
        tile = unit // across
        lanes = pl.ds(pl.multiple_of((unit - tile * across) * LANES, LANES), LANES)
        return tile * 8, lanes

    def rs_copy(chunk, unit):
        row, lanes = place_of(unit)
        return pltpu.make_async_remote_copy(
            src_ref=acc_ant.at[chunk, :, pl.ds(pl.multiple_of(row, 8), 8), lanes],
            dst_ref=rs_buf.at[chunk, me],
            send_sem=rs_send.at[chunk, unit], recv_sem=rs_recv.at[chunk, me],
            device_id=(owner_of(unit), band), device_id_type=MESH)

    def rs_arrival(chunk, source):
        return pltpu.make_async_remote_copy(
            src_ref=rs_buf.at[chunk, source], dst_ref=rs_buf.at[chunk, source],
            send_sem=rs_send.at[chunk, 0], recv_sem=rs_recv.at[chunk, source],
            device_id=(source, band), device_id_type=MESH)

    def ag_copy(chunk, unit, other):
        row, lanes = place_of(unit)
        block = gain.at[:, pl.ds(pl.multiple_of(chunk * CHK + row, 8), 8), lanes]
        return pltpu.make_async_remote_copy(
            src_ref=block, dst_ref=block,
            send_sem=ag_send.at[chunk, other], recv_sem=ag_recv.at[chunk, unit],
            device_id=(other, band), device_id_type=MESH)

    def units(body):
        def step(k, carry):
            unit = lax.rem(me + k, UNITS)

            @pl.when(owner_of(unit) != me)
            def _():
                body(unit)

            return carry

        lax.fori_loop(0, UNITS, step, 0)

    def send_sums(chunk):
        units(lambda unit: rs_copy(chunk, unit).start())

    def update_gains(chunk):
        @pl.when(i_own)
        def _():
            row, lanes = place_of(my_unit)
            rs_buf[chunk, me] = acc_ant[chunk, :, pl.ds(pl.multiple_of(row, 8), 8), lanes]
            others(lambda r: rs_arrival(chunk, grp_other(r)).wait_recv())
            total = rs_buf[chunk, 0]
            for source in range(1, N):
                total = total + rs_buf[chunk, source]
            share = 0.5 / (total[2] + RIDGE)
            here = pl.ds(pl.multiple_of(chunk * CHK + row, 8), 8)
            gain[0, here, lanes] = 0.5 * gain[0, here, lanes] + total[0] * share
            gain[1, here, lanes] = 0.5 * gain[1, here, lanes] + total[1] * share
            others(lambda r: ag_copy(chunk, my_unit, grp_other(r)).start())

    def await_gains(chunk):
        units(lambda unit: ag_copy(chunk, unit, owner_of(unit)).wait_recv())
        units(lambda unit: rs_copy(chunk, unit).wait_send())

        @pl.when(i_own)
        def _():
            others(lambda r: ag_copy(chunk, my_unit, grp_other(r)).wait_send())

    def mod_copy(source, other):
        return pltpu.make_async_remote_copy(
            src_ref=model_t.at[pl.ds(pl.multiple_of(other * OWN, OWN), OWN), :],
            dst_ref=model_band.at[:, pl.ds(pl.multiple_of(source * LANES, LANES), LANES)],
            send_sem=mod_send.at[other], recv_sem=mod_recv.at[source],
            device_id=(me, other), device_id_type=MESH)

    def iteration(s, carry):
        chunk = lax.rem(s, CHUNKS)

        @pl.when(s >= CHUNKS)
        def _():
            await_gains(chunk)

        group_fit(chunk)
        antenna_sums(chunk)

        @pl.when(s == 0)
        def _():
            pl.semaphore_wait(barrier, 2 * (N - 1))

        send_sums(chunk)

        @pl.when(s >= 1)
        def _():
            update_gains(lax.rem(s + CHUNKS - 1, CHUNKS))

        @pl.when(s == 0)
        def _():
            loads[5].wait()
            model = sky[0] * sky[0] + sky[1] * sky[1]
            square[CH:, :] = jnp.zeros((LANES - CH, LANES), f32)
            square[:CH, :] = model
            model_t[...] = square[...].T
            own_rows = pl.ds(pl.multiple_of(band * OWN, OWN), OWN)
            own_lanes = pl.ds(pl.multiple_of(band * LANES, LANES), LANES)
            model_band[:, own_lanes] = model_t[own_rows, :]
            others(lambda r: mod_copy(band, chan_other(r)).start())

        return carry

    lax.fori_loop(0, ITERS * CHUNKS, iteration, 0)

    def last(chunk, carry):
        await_gains(chunk)
        group_fit(chunk)

        @pl.when(chunk == 0)
        def _():
            update_gains(CHUNKS - 1)

        misfit(chunk)
        return carry

    lax.fori_loop(0, CHUNKS, last, 0)

    ur, ui = unique[0], unique[1]
    sr, si = sky[0], sky[1]
    ratio[:CH, :] = ur * sr + ui * si
    ratio[CH:, :] = ui * sr - ur * si
    loads[6].wait()
    part[...] = exact_dot(ahead[...], ratio[...]).T

    def cr_copy(source, other):
        return pltpu.make_async_remote_copy(
            src_ref=part.at[pl.ds(pl.multiple_of(other * OWN, OWN), OWN), :], dst_ref=coef_buf.at[source],
            send_sem=cr_send.at[other], recv_sem=cr_recv.at[source],
            device_id=(me, other), device_id_type=MESH)

    others(lambda r: cr_copy(band, chan_other(r)).start())
    coef_buf[band] = part[pl.ds(pl.multiple_of(band * OWN, OWN), OWN), :]

    gains_out[...] = gain[:, :, :ANT]
    east = vec_acc[0:1, :] / vec_acc[2:3, :]
    north = vec_acc[1:2, :] / vec_acc[2:3, :]
    square[...] = jnp.zeros_like(square)
    square[0:1, :] = east
    square[1:2, :] = north
    vec_t[...] = square[...].T
    model = sr * sr + si * si
    squared = model * model
    fields = [
        ur * ur + ui * ui, model, squared * (east * east), squared * (east * north),
        squared * (north * north), chi_acc[...],
    ]
    lane = lax.broadcasted_iota(jnp.int32, (CH, LANES), 1)
    table = jnp.zeros((CH, LANES), f32)
    for place, field in enumerate(fields):
        table = jnp.where(lane == place, jnp.sum(field, axis=1, keepdims=True), table)
    square[CH:, :] = jnp.zeros((LANES - CH, LANES), f32)
    square[:CH, :] = table
    local = square[...].T[:8, :]

    channel = band * CH + lax.broadcasted_iota(jnp.int32, (1, LANES), 1)
    frequency = 1.0 + channel.astype(f32) * (1.0 / CHANNEL_COUNT)
    squares = frequency * frequency
    slope_parts = squares * local[2:5]
    at = lax.broadcasted_iota(jnp.int32, (1, N * LANES), 1)
    band_channel = (at // LANES) * CH + lax.rem(at, LANES)
    band_frequency = 1.0 + band_channel.astype(f32) * (1.0 / CHANNEL_COUNT)
    my_groups = vec_t[pl.ds(pl.multiple_of(band * OWN, OWN), OWN), :]

    loads[7].wait()
    others(lambda r: mod_copy(chan_other(r), band).wait_recv())
    others(lambda r: mod_copy(band, chan_other(r)).wait_send())
    weights_east = model_band[...] * my_groups[:, 0:1]
    weights_north = model_band[...] * my_groups[:, 1:2]

    others(lambda r: cr_copy(chan_other(r), band).wait_recv())
    coef = coef_buf[0]
    for source in range(1, N):
        coef = coef + coef_buf[source]
    phases = exact_dot(coef, back[...])
    right_east = jnp.sum(weights_east * phases, axis=0, keepdims=True)
    right_north = jnp.sum(weights_north * phases, axis=0, keepdims=True)
    slope_east = jnp.sum(band_frequency * right_east, axis=1, keepdims=True)
    slope_north = jnp.sum(band_frequency * right_north, axis=1, keepdims=True)
    first_lane = lax.broadcasted_iota(jnp.int32, (1, LANES), 1) == 0
    slope_rows = jnp.concatenate(
        [jnp.where(first_lane, slope_east, 0.0), jnp.where(first_lane, slope_north, 0.0),
         slope_parts, jnp.zeros((1, LANES), f32)], axis=0)
    for other in range(N):
        lanes = slice(other * LANES, (other + 1) * LANES)
        band_send_buf[other] = jnp.concatenate([right_east[:, lanes], right_north[:, lanes], slope_rows], axis=0)

    def band_copy(source, other):
        return pltpu.make_async_remote_copy(
            src_ref=band_send_buf.at[other], dst_ref=band_buf.at[source],
            send_sem=band_send.at[other], recv_sem=band_recv.at[source],
            device_id=(me, other), device_id_type=MESH)

    others(lambda r: band_copy(band, chan_other(r)).start())
    band_buf[band] = band_send_buf[band]
    others(lambda r: cr_copy(band, chan_other(r)).wait_send())
    others(lambda r: band_copy(chan_other(r), band).wait_recv())
    sums = band_buf[0]
    for source in range(1, N):
        sums = sums + band_buf[source]

    tot_buf[me] = jnp.concatenate(
        [local[0:5], sums[0:2], local[5:6], sums[2:7], jnp.zeros((3, LANES), f32)], axis=0)

    def tot_copy(source, other):
        return pltpu.make_async_remote_copy(
            src_ref=tot_buf.at[source], dst_ref=tot_buf.at[source],
            send_sem=tot_send.at[other], recv_sem=tot_recv.at[source],
            device_id=(other, band), device_id_type=MESH)

    others(lambda r: tot_copy(me, grp_other(r)).start())
    others(lambda r: band_copy(band, chan_other(r)).wait_send())
    others(lambda r: tot_copy(grp_other(r), me).wait_recv())
    totals = tot_buf[0]
    for source in range(1, N):
        totals = totals + tot_buf[source]
    others(lambda r: tot_copy(me, grp_other(r)).wait_send())
    chi_out[...] = totals[7:8, :CH]

    terms = jnp.sum(totals[8:16], axis=1, keepdims=True)
    slope_east, slope_north = solve_pair(
        terms[2:3], terms[3:4], terms[4:5], terms[0:1], terms[1:2])
    tilt_east, tilt_north = solve_pair(
        totals[2:3], totals[3:4], totals[4:5], totals[5:6], totals[6:7])
    tilt_east = tilt_east - frequency * slope_east
    tilt_north = tilt_north - frequency * slope_north
    amplitude = jnp.sqrt((totals[0:1] + EPSILON) / (totals[1:2] + EPSILON))
    square[0:8, :] = jnp.concatenate(
        [frequency, tilt_east, tilt_north, 1.0 / amplitude, jnp.zeros((4, LANES), f32)], axis=0)
    columns = square[...].T[:CH, :]
    along = slope_east * east + slope_north * north
    turn = columns[:, 0:1] * along + columns[:, 1:2] * east + columns[:, 2:3] * north
    rotation_cos = jnp.cos(turn) * columns[:, 3:4]
    rotation_sin = jnp.sin(turn) * columns[:, 3:4]
    cal_out[0] = ur * rotation_cos + ui * rotation_sin
    cal_out[1] = ui * rotation_cos - ur * rotation_sin


def per_device(ahead, back, vis, ants, gid, sky, start, coords):
    vmem = pl.BlockSpec(memory_space=pltpu.VMEM)
    hbm = pl.BlockSpec(memory_space=pltpu.HBM)
    dma = pltpu.SemaphoreType.DMA
    gains, cal, chi = pl.pallas_call(
        kernel,
        out_shape=(
            jax.ShapeDtypeStruct((2, CH, ANT), f32),
            jax.ShapeDtypeStruct((2, CH, GRP), f32),
            jax.ShapeDtypeStruct((1, CH), f32),
        ),
        in_specs=[hbm] * 8,
        out_specs=(vmem, vmem, vmem),
        scratch_shapes=[
            pltpu.VMEM((2, CH, BL), f32),
            pltpu.VMEM((2, BL), jnp.int32),
            pltpu.VMEM((1, BL), jnp.int32),
            pltpu.VMEM((2, CH, GRP), f32),
            pltpu.VMEM((2, CH, ANT), f32),
            pltpu.VMEM((2, ANT), f32),
            pltpu.VMEM((2 * NDLY, 2 * CH), f32),
            pltpu.VMEM((2 * NDLY, N * LANES), f32),
            pltpu.VMEM((STEPS, ANT_PAD, 2 * TILE), bf16),
            pltpu.VMEM((STEPS, GRP, TILE), bf16),
            pltpu.VMEM((STEPS, 2 * CHK, 2 * TILE), f32),
            pltpu.VMEM((2, CH, ANT_PAD), f32),
            pltpu.VMEM((4 * CHK, ANT_PAD), bf16),
            pltpu.VMEM((6 * CHK, GRP), f32),
            pltpu.VMEM((2, CH, GRP), f32),
            pltpu.VMEM((4 * CHK, GRP), bf16),
            pltpu.VMEM((6 * CHK, ANT_PAD), f32),
            pltpu.VMEM((CHUNKS, 3, CHK, ANT_PAD), f32),
            pltpu.VMEM((CHUNKS, N, 3, 8, LANES), f32),
            pltpu.VMEM((2 * CH, GRP), f32),
            pltpu.VMEM((GRP, 2 * NDLY), f32),
            pltpu.VMEM((N, OWN, 2 * NDLY), f32),
            pltpu.VMEM((GRP, LANES), f32),
            pltpu.VMEM((OWN, N * LANES), f32),
            pltpu.VMEM((LANES, LANES), f32),
            pltpu.VMEM((8, GRP), f32),
            pltpu.VMEM((GRP, LANES), f32),
            pltpu.VMEM((CH, LANES), f32),
            pltpu.VMEM((N, 8, LANES), f32),
            pltpu.VMEM((N, 8, LANES), f32),
            pltpu.VMEM((N, 16, LANES), f32),
            dma((8,)),
            dma((CHUNKS, UNITS)), dma((CHUNKS, N)), dma((CHUNKS, N)), dma((CHUNKS, UNITS)),
        ] + [dma((N,))] * 8,
        compiler_params=pltpu.CompilerParams(
            collective_id=0, has_side_effects=True, vmem_limit_bytes=48 * 1024 * 1024),
        cost_estimate=pl.CostEstimate(flops=20_000_000_000, bytes_accessed=4_000_000, transcendentals=0),
    )(vis, ants, gid, sky, start, coords, ahead, back)
    return gains, cal, chi.reshape(CH)


def solution(mesh):
    ahead, back = delay_tables()

    def program(vis, ants, gid, sky, start, coords):
        return jax.shard_map(
            functools.partial(per_device, ahead, back),
            mesh=mesh,
            in_specs=(
                P(None, "chan", "grp"),
                P(None, "grp"),
                P("grp", None),
                P(None, "chan", "grp"),
                P(None, "chan", None),
                P(),
            ),
            out_specs=(P(None, "chan", None), P(None, "chan", "grp"), P("chan")),
            check_vma=False,
        )(vis, ants, gid, sky, start, coords)

    return program
```

time: 150 us -> 112 us (0.75)
  Pallas kernels: 139 us -> 101 us
    pallas_call x1, Pallas kernels: 139 us -> 101 us  [per_device(): pl.pallas_call(kernel, out_shape=(jax.ShapeDtypeStruct((2, CH, ANT), f32)...]
    unnamed x17 -> x19, local copies, waits for them, and re-layouts: 9.26 us -> 10 us
where the time goes in v2:
time: 112 us
  Pallas kernels  101 us (90%)
  local copies, waits for them, and re-layouts  10 us (9%)
    pallas_call x1, Pallas kernels, per_device(): pl.pallas_call(kernel, out_shape=(jax.ShapeDtypeStruct((2, CH, ANT), f32)...  101 us
    unnamed x19, local copies, waits for them, and re-layouts  10 us

profile of v2, /device:TPU:1, one launch (start us, length us, event | category | flops | bytes accessed | tf_op | source)
XLA Modules:
  0.0 112.1 jit_solution(7776223238736738284)
XLA Ops:
  0.6 0.0 copy-start
  0.6 1.4 %copy-done = f32[2,96,2048]{2,1,0:T(8,128)S(1)} copy-done((f32[2,96,2048]{2,1,0:T(8,128)S(1)}, f32[2,96,2048]{2,1,0:T(8,128)}, u32[]{:S(2)}) %copy-start) | copy-done | bytes 1572888
  2.0 0.0 copy-start.1
  2.0 1.0 copy-done.1
  3.0 0.0 copy-start.2
  3.0 0.9 copy-done.2
  3.9 0.0 copy-start.3
  3.9 0.7 copy-done.3
  4.6 0.0 copy-start.4
  4.6 0.7 copy-done.4
  5.3 0.0 copy-start.5
  5.3 0.7 copy-done.5
  6.0 0.0 copy-start.6
  6.0 1.6 %copy-done.6 = f32[16,128,192]{2,1,0:T(8,128)S(1)} copy-done((f32[16,128,192]{2,1,0:T(8,128)S(1)}, f32[16,128,192]{2,1,0:T(8,128)}, u32[]{:S(2)}) %copy-start.6) | copy-done | bytes 1572888
  7.6 0.0 copy-start.7
  7.6 1.2 %copy-done.7 = f32[128,2048]{1,0:T(8,128)S(1)} copy-done((f32[128,2048]{1,0:T(8,128)S(1)}, f32[128,2048]{1,0:T(8,128)}, u32[]{:S(2)}) %copy-start.7) | copy-done | bytes 1048600
  8.8 101.4 %shard_map.103 = (f32[2,96,350]{2,1,0:T(8,128)S(1)}, f32[2,96,128]{2,1,0:T(8,128)S(1)}, f32[1,96]{1,0:T(1,128)S(1)}) custom-call(f32[2,96,2048]{2,1,0:T(8,128)S(1)} %copy-done, s32[2,2048]{1,0:T(2,128)S(1)} %copy-done.3, s32[1,2048]{1,0:T(1,128)S(1)} %copy-done.4, f32[2,96,128]{2,1,0:T(8,128)S(1)} %copy-done.2, f32[2,96,350]{2,1,0:T(8,128)S(1)} %copy-done.1, ...), custom_call_target="tpu_custom_call" | custom-call | flops 20000000000 | bytes 4000000 | tf_op jit(solution)/shard_map/pallas_call | solution.py:486
  110.2 0.7 copy.14
  110.9 0.6 copy.15
  111.6 0.5 copy.16
Async XLA Ops:
  0.6 1.4 %copy-start = (f32[2,96,2048]{2,1,0:T(8,128)S(1)}, f32[2,96,2048]{2,1,0:T(8,128)}, u32[]{:S(2)}) copy-start(f32[2,96,2048]{2,1,0:T(8,128)} %vis_hbm.1) | copy-start | bytes 4718596
  2.0 1.0 copy-start.1
  3.0 0.9 copy-start.2
  3.9 0.7 copy-start.3
  4.6 0.7 copy-start.4
  5.3 0.7 copy-start.5
  6.0 1.6 %copy-start.6 = (f32[16,128,192]{2,1,0:T(8,128)S(1)}, f32[16,128,192]{2,1,0:T(8,128)}, u32[]{:S(2)}) copy-start(f32[16,128,192]{2,1,0:T(8,128)} %constant.4.clone.ahead_hbm) | copy-start | bytes 4718596
  7.6 1.2 %copy-start.7 = (f32[128,2048]{1,0:T(8,128)S(1)}, f32[128,2048]{1,0:T(8,128)}, u32[]{:S(2)}) copy-start(f32[128,2048]{1,0:T(8,128)} %constant.5.clone.back_hbm) | copy-start | bytes 3145732

commit v3 on v2

--- a/solution.py
+++ b/solution.py
@@ -24,9 +24,17 @@
 GRP = 128
 TILE = 256
 STEPS = BL // TILE
+SPAN = 8
 OWN = GRP // N
 LANES = 128
 UNITS = (CHK // 8) * (ANT_PAD // LANES)
+
+GRP_STEPS = sorted(
+    ((dx, dy) for dx in range(4) for dy in range(4) if dx or dy),
+    key=lambda step: -min(step[0], 4 - step[0]) - min(step[1], 4 - step[1]))
+CHAN_STEPS = sorted(
+    ((dz, core) for dz in range(8) for core in range(2) if dz or core),
+    key=lambda step: -2 * min(step[0], 8 - step[0]) - step[1])
 
 MESH = pl.DeviceIdType.MESH
 HIGHEST = lax.Precision.HIGHEST
@@ -91,7 +99,7 @@
     vis_hbm, ants_hbm, gid_hbm, sky_hbm, start_hbm, coords_hbm, ahead_hbm, back_hbm,
     gains_out, cal_out, chi_out,
     vis, ants, gid, sky, start, coords, ahead, back,
-    hot, grp_hot, pair, gain, gain2, acc_grp, unique, unique2, acc_sum, acc_ant, rs_buf,
+    hot, grp_hot, hot_t, grp_hot_t, rows_a, rows_b, pair, gain, gain2, acc_grp, unique, unique2, acc_sum, acc_ant, rs_buf,
     ratio, part, coef_buf, model_t, model_band, square, vec_acc, vec_t, chi_acc,
     band_send_buf, band_buf, tot_buf,
     load_sem, rs_send, rs_recv, ag_send, ag_recv, mod_send, mod_recv, cr_send, cr_recv,
@@ -107,10 +115,14 @@
             body(r)
 
     def grp_other(r):
-        return lax.rem(me + r, N)
+        dx, dy = GRP_STEPS[r - 1]
+        x = me // 4
+        return lax.rem(x + dx, 4) * 4 + lax.rem(me - 4 * x + dy, 4)
 
     def chan_other(r):
-        return lax.rem(band + r, N)
+        dz, core = CHAN_STEPS[r - 1]
+        z = band // 2
+        return lax.rem(z + dz, 8) * 2 + lax.rem(band - 2 * z + core, 2)
 
     loads = [
         pltpu.make_async_copy(ants_hbm, ants, load_sem.at[0]),
@@ -152,13 +164,17 @@
         hot[t, :, :TILE] = p_hot
         hot[t, :, TILE:] = q_hot
         grp_hot[t] = g_hot
+        here = pl.multiple_of(2 * t * TILE, TILE)
+        hot_t[pl.ds(here, TILE), :] = p_hot.T
+        hot_t[pl.ds(here + TILE, TILE), :] = q_hot.T
+        grp_hot_t[cols, :] = g_hot.T
         place = joined(dot(places, p_hot - q_hot))
         row = lax.broadcasted_iota(jnp.int32, place.shape, 0)
         place = jnp.where(row == 2, 1.0, place)
         vec_acc[...] += joined(dot_last(two_parts(place), g_hot))
         return carry
 
-    lax.fori_loop(0, STEPS, build, 0)
+    lax.fori_loop(0, STEPS, build, 0, unroll=STEPS)
 
     loads[3].wait()
     gain[:, :, :ANT] = start[...]
@@ -170,10 +186,9 @@
     def group_fit(chunk):
         mine = rows_of(chunk)
         gain2[...] = two_parts(gain[:, mine, :].reshape(2 * CHK, ANT_PAD))
-        acc_grp[...] = jnp.zeros_like(acc_grp)
-
-        def step(t, carry):
-            cols = pl.ds(pl.multiple_of(t * TILE, TILE), TILE)
+
+        for t in range(STEPS):
+            cols = slice(t * TILE, (t + 1) * TILE)
             pq = joined(dot(gain2[...], hot[t]))
             pair[t] = pq
             a, b = pq[:CHK, :TILE], pq[CHK:, :TILE]
@@ -182,10 +197,11 @@
             wr = a * c + b * d
             wi = b * c - a * d
             rows = jnp.concatenate([x * wr + y * wi, y * wr - x * wi, wr * wr + wi * wi], axis=0)
-            acc_grp[...] += dot_last(two_parts(rows), grp_hot[t])
-            return carry
-
-        lax.fori_loop(0, STEPS, step, 0, unroll=8)
+            rows_a[:, cols] = two_parts(rows)
+            if (t + 1) % SPAN == 0:
+                part_cols = slice((t + 1 - SPAN) * TILE, (t + 1) * TILE)
+                acc_grp[...] = dot(rows_a[:, part_cols], grp_hot_t[part_cols, :])
+
         sums = joined(acc_grp[...])
         scale = 1.0 / (sums[2 * CHK:] + RIDGE)
         ur, ui = sums[:CHK] * scale, sums[CHK:2 * CHK] * scale
@@ -195,10 +211,9 @@
 
     def antenna_sums(chunk):
         mine = rows_of(chunk)
-        acc_sum[...] = jnp.zeros_like(acc_sum)
-
-        def step(t, carry):
-            cols = pl.ds(pl.multiple_of(t * TILE, TILE), TILE)
+
+        for t in range(STEPS):
+            cols = slice(t * TILE, (t + 1) * TILE)
             uu = joined(dot(unique2[...], grp_hot[t]))
             s, v = uu[:CHK], uu[CHK:]
             pq = pair[t]
@@ -210,10 +225,12 @@
             size = s * s + v * v
             for_p = jnp.concatenate([c * zr - d * zi, c * zi + d * zr, size * (c * c + d * d)], axis=0)
             for_q = jnp.concatenate([a * zr + b * zi, b * zr - a * zi, size * (a * a + b * b)], axis=0)
-            acc_sum[...] += dot_last(two_parts(jnp.concatenate([for_p, for_q], axis=1)), hot[t])
-            return carry
-
-        lax.fori_loop(0, STEPS, step, 0, unroll=8)
+            rows_b[:, 2 * t * TILE:(2 * t + 1) * TILE] = two_parts(for_p)
+            rows_b[:, (2 * t + 1) * TILE:(2 * t + 2) * TILE] = two_parts(for_q)
+            if (t + 1) % SPAN == 0:
+                part_cols = slice(2 * (t + 1 - SPAN) * TILE, 2 * (t + 1) * TILE)
+                acc_sum[...] = dot(rows_b[:, part_cols], hot_t[part_cols, :])
+
         acc_ant[chunk] = joined(acc_sum[...]).reshape(3, CHK, ANT_PAD)
 
     def misfit(chunk):
@@ -235,7 +252,7 @@
             chi_acc[mine, :] += e[:, :LANES] + e[:, LANES:]
             return carry
 
-        lax.fori_loop(0, STEPS, step, 0, unroll=8)
+        lax.fori_loop(0, STEPS, step, 0, unroll=STEPS)
 
     def place_of(unit):
         across = ANT_PAD // LANES
@@ -266,16 +283,14 @@
             device_id=(other, band), device_id_type=MESH)
 
     def units(body):
-        def step(k, carry):
-            unit = lax.rem(me + k, UNITS)
-
-            @pl.when(owner_of(unit) != me)
+        def one(r):
+            other = grp_other(r)
+
+            @pl.when(lax.rem(other, 5) != 0)
             def _():
-                body(unit)
-
-            return carry
-
-        lax.fori_loop(0, UNITS, step, 0)
+                body(other - 1 - other // 5)
+
+        others(one)
 
     def send_sums(chunk):
         units(lambda unit: rs_copy(chunk, unit).start())
@@ -503,6 +518,10 @@
             pltpu.VMEM((2 * NDLY, N * LANES), f32),
             pltpu.VMEM((STEPS, ANT_PAD, 2 * TILE), bf16),
             pltpu.VMEM((STEPS, GRP, TILE), bf16),
+            pltpu.VMEM((2 * BL, ANT_PAD), bf16),
+            pltpu.VMEM((BL, GRP), bf16),
+            pltpu.VMEM((6 * CHK, BL), bf16),
+            pltpu.VMEM((6 * CHK, 2 * BL), bf16),
             pltpu.VMEM((STEPS, 2 * CHK, 2 * TILE), f32),
             pltpu.VMEM((2, CH, ANT_PAD), f32),
             pltpu.VMEM((4 * CHK, ANT_PAD), bf16),
@@ -528,7 +547,7 @@
             dma((CHUNKS, UNITS)), dma((CHUNKS, N)), dma((CHUNKS, N)), dma((CHUNKS, UNITS)),
         ] + [dma((N,))] * 8,
         compiler_params=pltpu.CompilerParams(
-            collective_id=0, has_side_effects=True, vmem_limit_bytes=48 * 1024 * 1024),
+            collective_id=0, has_side_effects=True, vmem_limit_bytes=60 * 1024 * 1024),
         cost_estimate=pl.CostEstimate(flops=20_000_000_000, bytes_accessed=4_000_000, transcendentals=0),
     )(vis, ants, gid, sky, start, coords, ahead, back)
     return gains, cal, chi.reshape(CH)

time: 112 us -> 93 us (0.83)
  Pallas kernels: 101 us -> 87.9 us
  local copies, waits for them, and re-layouts: 10 us -> 4.35 us
    pallas_call x1, Pallas kernels: 101 us -> 87.9 us  [per_device(): pl.pallas_call(kernel, out_shape=(jax.ShapeDtypeStruct((2, CH, ANT), f32)...]
    unnamed x19 -> x3, local copies, waits for them, and re-layouts: 10 us -> 4.35 us
where the time goes in v3:
time: 93 us; the launch traced here: 92.9 us
  Pallas kernels  87.9 us (95%)
  local copies, waits for them, and re-layouts  4.35 us (5%)
    pallas_call x1, Pallas kernels, per_device(): pl.pallas_call(kernel, out_shape=(jax.ShapeDtypeStruct((2, CH, ANT), f32)...  87.9 us
    unnamed x3, local copies, waits for them, and re-layouts  4.35 us

profile of v3, /device:TPU:1, one launch (start us, length us, event | category | flops | bytes accessed | tf_op | source)
XLA Modules:
  0.0 92.9 jit_solution(9954011893976453492)
XLA Ops:
  0.6 87.9 %shard_map.103 = (f32[2,96,350]{2,1,0:T(8,128)}, f32[2,96,128]{2,1,0:T(8,128)}, f32[1,96]{1,0:T(1,128)}) custom-call(f32[2,96,2048]{2,1,0:T(8,128)} %vis_hbm.1, s32[2,2048]{1,0:T(2,128)} %ants_hbm.1, s32[1,2048]{1,0:T(1,128)} %gid_hbm.1, f32[2,96,128]{2,1,0:T(8,128)} %sky_hbm.1, f32[2,96,350]{2,1,0:T(8,128)} %start_hbm.1, f32[2,350]{1,0:T(2,128)} %coords_hbm.1, ...), custom_call_target="tpu_custom_call" | custom-call | flops 20000000000 | bytes 4000000 | tf_op jit(solution)/shard_map/pallas_call | solution.py:501
  88.5 1.7 %copy.14 = f32[2,96,350]{2,1,0:T(8,128)} copy(f32[2,96,350]{2,1,0:T(8,128)} %get-tuple-element.12) | data formatting | bytes 537600
  90.2 1.5 %copy.15 = f32[2,96,128]{2,1,0:T(8,128)} copy(f32[2,96,128]{2,1,0:T(8,128)} %get-tuple-element.13) | data formatting | bytes 196608
  91.8 1.1 %copy.16 = f32[96]{0:T(128)} copy(f32[96]{0:T(128)} %bitcast.1) | data formatting | bytes 768

commit v4 on v3

--- a/solution.py
+++ b/solution.py
@@ -37,7 +37,6 @@
     key=lambda step: -2 * min(step[0], 8 - step[0]) - step[1])
 
 MESH = pl.DeviceIdType.MESH
-HIGHEST = lax.Precision.HIGHEST
 f32 = jnp.float32
 bf16 = jnp.bfloat16
 
@@ -63,10 +62,6 @@
 
 def dot_last(left, right):
     return lax.dot_general(left, right, (((1,), (1,)), ((), ())), preferred_element_type=f32)
-
-
-def exact_dot(left, right):
-    return jnp.dot(left, right, precision=HIGHEST, preferred_element_type=f32)
 
 
 def solve_pair(entry_xx, entry_xy, entry_yy, right_x, right_y):
@@ -92,7 +87,14 @@
     back = np.zeros((2 * NDLY, N, LANES))
     back[:NDLY, :, :CH] = sines.transpose(1, 0, 2)
     back[NDLY:, :, :CH] = cosines.transpose(1, 0, 2)
-    return (ahead / CHANNEL_COUNT).astype(np.float32), back.reshape(2 * NDLY, N * LANES).astype(np.float32)
+    ahead = ahead / CHANNEL_COUNT
+    back = back.reshape(2 * NDLY, N * LANES)
+    ahead_1, back_1 = ahead.astype(bf16), back.astype(bf16)
+    ahead_2 = (ahead - ahead_1.astype(np.float64)).astype(bf16)
+    back_2 = (back - back_1.astype(np.float64)).astype(bf16)
+    ahead = np.concatenate(
+        [np.concatenate([ahead_1, ahead_1], axis=2), np.concatenate([ahead_2, ahead_2], axis=2)], axis=1)
+    return ahead, np.concatenate([back_1, back_2], axis=0)
 
 
 def kernel(
@@ -129,10 +131,14 @@
         pltpu.make_async_copy(gid_hbm, gid, load_sem.at[1]),
         pltpu.make_async_copy(coords_hbm, coords, load_sem.at[2]),
         pltpu.make_async_copy(start_hbm, start, load_sem.at[3]),
-        pltpu.make_async_copy(vis_hbm, vis, load_sem.at[4]),
+        pltpu.make_async_copy(vis_hbm.at[:, 0:CHK], vis.at[:, 0:CHK], load_sem.at[4]),
         pltpu.make_async_copy(sky_hbm, sky, load_sem.at[5]),
         pltpu.make_async_copy(ahead_hbm.at[band], ahead, load_sem.at[6]),
         pltpu.make_async_copy(back_hbm, back, load_sem.at[7]),
+    ] + [
+        pltpu.make_async_copy(
+            vis_hbm.at[:, c * CHK:(c + 1) * CHK], vis.at[:, c * CHK:(c + 1) * CHK], load_sem.at[7 + c])
+        for c in range(1, CHUNKS)
     ]
     for load in loads:
         load.start()
@@ -265,21 +271,18 @@
         return pltpu.make_async_remote_copy(
             src_ref=acc_ant.at[chunk, :, pl.ds(pl.multiple_of(row, 8), 8), lanes],
             dst_ref=rs_buf.at[chunk, me],
-            send_sem=rs_send.at[chunk, unit], recv_sem=rs_recv.at[chunk, me],
+            send_sem=rs_send.at[chunk], recv_sem=rs_recv.at[chunk],
             device_id=(owner_of(unit), band), device_id_type=MESH)
 
-    def rs_arrival(chunk, source):
-        return pltpu.make_async_remote_copy(
-            src_ref=rs_buf.at[chunk, source], dst_ref=rs_buf.at[chunk, source],
-            send_sem=rs_send.at[chunk, 0], recv_sem=rs_recv.at[chunk, source],
-            device_id=(source, band), device_id_type=MESH)
+    def arrivals(sem, shape):
+        return pltpu.make_async_copy(shape, shape, sem)
 
     def ag_copy(chunk, unit, other):
         row, lanes = place_of(unit)
         block = gain.at[:, pl.ds(pl.multiple_of(chunk * CHK + row, 8), 8), lanes]
         return pltpu.make_async_remote_copy(
             src_ref=block, dst_ref=block,
-            send_sem=ag_send.at[chunk, other], recv_sem=ag_recv.at[chunk, unit],
+            send_sem=ag_send.at[chunk], recv_sem=ag_recv.at[chunk],
             device_id=(other, band), device_id_type=MESH)
 
     def units(body):
@@ -300,7 +303,7 @@
         def _():
             row, lanes = place_of(my_unit)
             rs_buf[chunk, me] = acc_ant[chunk, :, pl.ds(pl.multiple_of(row, 8), 8), lanes]
-            others(lambda r: rs_arrival(chunk, grp_other(r)).wait_recv())
+            arrivals(rs_recv.at[chunk], rs_buf.at[chunk, 0:N - 1]).wait()
             total = rs_buf[chunk, 0]
             for source in range(1, N):
                 total = total + rs_buf[chunk, source]
@@ -310,13 +313,24 @@
             gain[1, here, lanes] = 0.5 * gain[1, here, lanes] + total[1] * share
             others(lambda r: ag_copy(chunk, my_unit, grp_other(r)).start())
 
+    def by_place(body):
+        @pl.when(i_own)
+        def _():
+            body(UNITS - 1)
+
+        @pl.when(jnp.logical_not(i_own))
+        def _():
+            body(UNITS)
+
     def await_gains(chunk):
-        units(lambda unit: ag_copy(chunk, unit, owner_of(unit)).wait_recv())
-        units(lambda unit: rs_copy(chunk, unit).wait_send())
+        by_place(lambda n: arrivals(ag_recv.at[chunk], rs_buf.at[chunk, 0:n, 0:2]).wait())
+
+    def settle(chunk):
+        by_place(lambda n: arrivals(rs_send.at[chunk], rs_buf.at[chunk, 0:n]).wait())
 
         @pl.when(i_own)
         def _():
-            others(lambda r: ag_copy(chunk, my_unit, grp_other(r)).wait_send())
+            arrivals(ag_send.at[chunk], rs_buf.at[chunk, 0:N - 1, 0:2]).wait()
 
     def mod_copy(source, other):
         return pltpu.make_async_remote_copy(
@@ -332,7 +346,17 @@
         def _():
             await_gains(chunk)
 
+        for c in range(1, CHUNKS):
+            @pl.when(s == c)
+            def _():
+                loads[7 + c].wait()
+
         group_fit(chunk)
+
+        @pl.when(s >= CHUNKS)
+        def _():
+            settle(chunk)
+
         antenna_sums(chunk)
 
         @pl.when(s == 0)
@@ -341,11 +365,7 @@
 
         send_sums(chunk)
 
-        @pl.when(s >= 1)
-        def _():
-            update_gains(lax.rem(s + CHUNKS - 1, CHUNKS))
-
-        @pl.when(s == 0)
+        @pl.when(s == CHUNKS - 1)
         def _():
             loads[5].wait()
             model = sky[0] * sky[0] + sky[1] * sky[1]
@@ -357,6 +377,10 @@
             model_band[:, own_lanes] = model_t[own_rows, :]
             others(lambda r: mod_copy(band, chan_other(r)).start())
 
+        @pl.when(s >= 1)
+        def _():
+            update_gains(lax.rem(s + CHUNKS - 1, CHUNKS))
+
         return carry
 
     lax.fori_loop(0, ITERS * CHUNKS, iteration, 0)
@@ -365,11 +389,16 @@
         await_gains(chunk)
         group_fit(chunk)
 
+        settle(chunk)
+
         @pl.when(chunk == 0)
         def _():
             update_gains(CHUNKS - 1)
 
-        misfit(chunk)
+        @pl.when(chunk < CHUNKS - 1)
+        def _():
+            misfit(chunk)
+
         return carry
 
     lax.fori_loop(0, CHUNKS, last, 0)
@@ -379,7 +408,7 @@
     ratio[:CH, :] = ur * sr + ui * si
     ratio[CH:, :] = ui * sr - ur * si
     loads[6].wait()
-    part[...] = exact_dot(ahead[...], ratio[...]).T
+    part[...] = joined(dot(ahead[...], two_parts(ratio[...]))).T
 
     def cr_copy(source, other):
         return pltpu.make_async_remote_copy(
@@ -389,6 +418,7 @@
 
     others(lambda r: cr_copy(band, chan_other(r)).start())
     coef_buf[band] = part[pl.ds(pl.multiple_of(band * OWN, OWN), OWN), :]
+    misfit(CHUNKS - 1)
 
     gains_out[...] = gain[:, :, :ANT]
     east = vec_acc[0:1, :] / vec_acc[2:3, :]
@@ -430,7 +460,8 @@
     coef = coef_buf[0]
     for source in range(1, N):
         coef = coef + coef_buf[source]
-    phases = exact_dot(coef, back[...])
+    coef = two_parts(coef)
+    phases = joined(dot(jnp.concatenate([coef, coef], axis=1), back[...]))
     right_east = jnp.sum(weights_east * phases, axis=0, keepdims=True)
     right_north = jnp.sum(weights_north * phases, axis=0, keepdims=True)
     slope_east = jnp.sum(band_frequency * right_east, axis=1, keepdims=True)
@@ -514,8 +545,8 @@
             pltpu.VMEM((2, CH, GRP), f32),
             pltpu.VMEM((2, CH, ANT), f32),
             pltpu.VMEM((2, ANT), f32),
-            pltpu.VMEM((2 * NDLY, 2 * CH), f32),
-            pltpu.VMEM((2 * NDLY, N * LANES), f32),
+            pltpu.VMEM((4 * NDLY, 4 * CH), bf16),
+            pltpu.VMEM((4 * NDLY, N * LANES), bf16),
             pltpu.VMEM((STEPS, ANT_PAD, 2 * TILE), bf16),
             pltpu.VMEM((STEPS, GRP, TILE), bf16),
             pltpu.VMEM((2 * BL, ANT_PAD), bf16),
@@ -543,8 +574,8 @@
             pltpu.VMEM((N, 8, LANES), f32),
             pltpu.VMEM((N, 8, LANES), f32),
             pltpu.VMEM((N, 16, LANES), f32),
-            dma((8,)),
-            dma((CHUNKS, UNITS)), dma((CHUNKS, N)), dma((CHUNKS, N)), dma((CHUNKS, UNITS)),
+            dma((7 + CHUNKS,)),
+            dma((CHUNKS,)), dma((CHUNKS,)), dma((CHUNKS,)), dma((CHUNKS,)),
         ] + [dma((N,))] * 8,
         compiler_params=pltpu.CompilerParams(
             collective_id=0, has_side_effects=True, vmem_limit_bytes=60 * 1024 * 1024),

time: 93 us -> 90 us (0.968)
  Pallas kernels: 87.9 us -> 84.8 us
    pallas_call x1, Pallas kernels: 87.9 us -> 84.8 us  [per_device(): pl.pallas_call(kernel, out_shape=(jax.ShapeDtypeStruct((2, CH, ANT), f32)...]
where the time goes in v4:
time: 90 us; the launch traced here: 89.8 us
  Pallas kernels  84.8 us (94%)
  local copies, waits for them, and re-layouts  4.35 us (5%)
    pallas_call x1, Pallas kernels, per_device(): pl.pallas_call(kernel, out_shape=(jax.ShapeDtypeStruct((2, CH, ANT), f32)...  84.8 us
    unnamed x3, local copies, waits for them, and re-layouts  4.35 us

profile of v4, /device:TPU:1, one launch (start us, length us, event | category | flops | bytes accessed | tf_op | source)
XLA Modules:
  0.0 89.8 jit_solution(8591922748815321686)
XLA Ops:
  0.6 84.8 %shard_map.103 = (f32[2,96,350]{2,1,0:T(8,128)}, f32[2,96,128]{2,1,0:T(8,128)}, f32[1,96]{1,0:T(1,128)}) custom-call(f32[2,96,2048]{2,1,0:T(8,128)} %vis_hbm.1, s32[2,2048]{1,0:T(2,128)} %ants_hbm.1, s32[1,2048]{1,0:T(1,128)} %gid_hbm.1, f32[2,96,128]{2,1,0:T(8,128)} %sky_hbm.1, f32[2,96,350]{2,1,0:T(8,128)} %start_hbm.1, f32[2,350]{1,0:T(2,128)} %coords_hbm.1, ...), custom_call_target="tpu_custom_call" | custom-call | flops 20000000000 | bytes 4000000 | tf_op jit(solution)/shard_map/pallas_call | solution.py:532
  85.5 1.7 %copy.14 = f32[2,96,350]{2,1,0:T(8,128)} copy(f32[2,96,350]{2,1,0:T(8,128)} %get-tuple-element.12) | data formatting | bytes 537600
  87.2 1.5 %copy.15 = f32[2,96,128]{2,1,0:T(8,128)} copy(f32[2,96,128]{2,1,0:T(8,128)} %get-tuple-element.13) | data formatting | bytes 196608
  88.7 1.1 %copy.16 = f32[96]{0:T(128)} copy(f32[96]{0:T(128)} %bitcast.1) | data formatting | bytes 768

commit v5 on v4

--- a/solution.py
+++ b/solution.py
@@ -35,6 +35,8 @@
 CHAN_STEPS = sorted(
     ((dz, core) for dz in range(8) for core in range(2) if dz or core),
     key=lambda step: -2 * min(step[0], 8 - step[0]) - step[1])
+
+ACROSS = ANT_PAD // LANES
 
 MESH = pl.DeviceIdType.MESH
 f32 = jnp.float32
@@ -101,11 +103,10 @@
     vis_hbm, ants_hbm, gid_hbm, sky_hbm, start_hbm, coords_hbm, ahead_hbm, back_hbm,
     gains_out, cal_out, chi_out,
     vis, ants, gid, sky, start, coords, ahead, back,
-    hot, grp_hot, hot_t, grp_hot_t, rows_a, rows_b, pair, gain, gain2, acc_grp, unique, unique2, acc_sum, acc_ant, rs_buf,
+    hot, grp_hot, hot_t, grp_hot_t, rows_a, rows_b, pair, gain, wide, gain2, acc_grp, unique, unique2, acc_sum, acc_ant, rs_buf,
     ratio, part, coef_buf, model_t, model_band, square, vec_acc, vec_t, chi_acc,
     band_send_buf, band_buf, tot_buf,
-    load_sem, rs_send, rs_recv, ag_send, ag_recv, mod_send, mod_recv, cr_send, cr_recv,
-    band_send, band_recv, tot_send, tot_recv,
+    load_sem, rs_send, rs_recv, ag_send, ag_recv, mod_sem, cr_sem, band_sem, tot_sem,
 ):
     me = lax.axis_index("grp")
     band = lax.axis_index("chan")
@@ -151,14 +152,14 @@
 
     others(greet)
 
+    vec_acc[...] = jnp.zeros_like(vec_acc)
+    wide[:, :, ANT_PAD - LANES:] = jnp.zeros((2, CH, LANES), f32)
+    wide[0, :8, :] = jnp.zeros((8, ANT_PAD), f32)
     loads[0].wait()
     loads[1].wait()
     loads[2].wait()
-    vec_acc[...] = jnp.zeros_like(vec_acc)
-    gain[:, :, ANT_PAD - LANES:] = jnp.zeros((2, CH, LANES), f32)
-    gain[0, :8, :] = jnp.zeros((8, ANT_PAD), f32)
-    gain[0, 0:2, :ANT] = coords[...]
-    places = two_parts(gain[0, :8, :])
+    wide[0, 0:2, :ANT] = coords[...]
+    places = two_parts(wide[0, :8, :])
 
     def build(t, carry):
         cols = pl.ds(pl.multiple_of(t * TILE, TILE), TILE)
@@ -183,7 +184,11 @@
     lax.fori_loop(0, STEPS, build, 0, unroll=STEPS)
 
     loads[3].wait()
-    gain[:, :, :ANT] = start[...]
+    wide[:, :, :ANT] = start[...]
+    for chunk in range(CHUNKS):
+        for unit in range(UNITS):
+            row, lane = chunk * CHK + unit // ACROSS * 8, unit % ACROSS * LANES
+            gain[chunk, unit] = wide[:, row:row + 8, lane:lane + LANES]
     loads[4].wait()
 
     def rows_of(chunk):
@@ -191,7 +196,9 @@
 
     def group_fit(chunk):
         mine = rows_of(chunk)
-        gain2[...] = two_parts(gain[:, mine, :].reshape(2 * CHK, ANT_PAD))
+        gain2[...] = two_parts(jnp.concatenate(
+            [jnp.concatenate([gain[chunk, tile * ACROSS + l, q] for l in range(ACROSS)], axis=1)
+             for q in range(2) for tile in range(CHK // 8)], axis=0))
 
         for t in range(STEPS):
             cols = slice(t * TILE, (t + 1) * TILE)
@@ -237,7 +244,10 @@
                 part_cols = slice(2 * (t + 1 - SPAN) * TILE, 2 * (t + 1) * TILE)
                 acc_sum[...] = dot(rows_b[:, part_cols], hot_t[part_cols, :])
 
-        acc_ant[chunk] = joined(acc_sum[...]).reshape(3, CHK, ANT_PAD)
+        sums = joined(acc_sum[...]).reshape(3, CHK, ANT_PAD)
+        for unit in range(UNITS):
+            row, lane = unit // ACROSS * 8, unit % ACROSS * LANES
+            acc_ant[chunk, unit] = sums[:, row:row + 8, lane:lane + LANES]
 
     def misfit(chunk):
         mine = rows_of(chunk)
@@ -260,16 +270,9 @@
 
         lax.fori_loop(0, STEPS, step, 0, unroll=STEPS)
 
-    def place_of(unit):
-        across = ANT_PAD // LANES
-        tile = unit // across
-        lanes = pl.ds(pl.multiple_of((unit - tile * across) * LANES, LANES), LANES)
-        return tile * 8, lanes
-
     def rs_copy(chunk, unit):
-        row, lanes = place_of(unit)
         return pltpu.make_async_remote_copy(
-            src_ref=acc_ant.at[chunk, :, pl.ds(pl.multiple_of(row, 8), 8), lanes],
+            src_ref=acc_ant.at[chunk, unit],
             dst_ref=rs_buf.at[chunk, me],
             send_sem=rs_send.at[chunk], recv_sem=rs_recv.at[chunk],
             device_id=(owner_of(unit), band), device_id_type=MESH)
@@ -278,10 +281,8 @@
         return pltpu.make_async_copy(shape, shape, sem)
 
     def ag_copy(chunk, unit, other):
-        row, lanes = place_of(unit)
-        block = gain.at[:, pl.ds(pl.multiple_of(chunk * CHK + row, 8), 8), lanes]
         return pltpu.make_async_remote_copy(
-            src_ref=block, dst_ref=block,
+            src_ref=gain.at[chunk, unit], dst_ref=gain.at[chunk, unit],
             send_sem=ag_send.at[chunk], recv_sem=ag_recv.at[chunk],
             device_id=(other, band), device_id_type=MESH)
 
@@ -301,16 +302,13 @@
     def update_gains(chunk):
         @pl.when(i_own)
         def _():
-            row, lanes = place_of(my_unit)
-            rs_buf[chunk, me] = acc_ant[chunk, :, pl.ds(pl.multiple_of(row, 8), 8), lanes]
+            rs_buf[chunk, me] = acc_ant[chunk, my_unit]
             arrivals(rs_recv.at[chunk], rs_buf.at[chunk, 0:N - 1]).wait()
             total = rs_buf[chunk, 0]
             for source in range(1, N):
                 total = total + rs_buf[chunk, source]
             share = 0.5 / (total[2] + RIDGE)
-            here = pl.ds(pl.multiple_of(chunk * CHK + row, 8), 8)
-            gain[0, here, lanes] = 0.5 * gain[0, here, lanes] + total[0] * share
-            gain[1, here, lanes] = 0.5 * gain[1, here, lanes] + total[1] * share
+            gain[chunk, my_unit] = 0.5 * gain[chunk, my_unit] + total[:2] * share
             others(lambda r: ag_copy(chunk, my_unit, grp_other(r)).start())
 
     def by_place(body):
@@ -336,7 +334,7 @@
         return pltpu.make_async_remote_copy(
             src_ref=model_t.at[pl.ds(pl.multiple_of(other * OWN, OWN), OWN), :],
             dst_ref=model_band.at[:, pl.ds(pl.multiple_of(source * LANES, LANES), LANES)],
-            send_sem=mod_send.at[other], recv_sem=mod_recv.at[source],
+            send_sem=mod_sem.at[0], recv_sem=mod_sem.at[1],
             device_id=(me, other), device_id_type=MESH)
 
     def iteration(s, carry):
@@ -377,9 +375,19 @@
             model_band[:, own_lanes] = model_t[own_rows, :]
             others(lambda r: mod_copy(band, chan_other(r)).start())
 
-        @pl.when(s >= 1)
+        final = ITERS * CHUNKS - 1
+
+        @pl.when(jnp.logical_and(s >= 1, s <= final - CHUNKS + 1))
         def _():
             update_gains(lax.rem(s + CHUNKS - 1, CHUNKS))
+
+        @pl.when(s == final)
+        def _():
+            def each(c, carry):
+                update_gains(c)
+                return carry
+
+            lax.fori_loop(0, CHUNKS, each, 0)
 
         return carry
 
@@ -390,10 +398,6 @@
         group_fit(chunk)
 
         settle(chunk)
-
-        @pl.when(chunk == 0)
-        def _():
-            update_gains(CHUNKS - 1)
 
         @pl.when(chunk < CHUNKS - 1)
         def _():
@@ -413,14 +417,18 @@
     def cr_copy(source, other):
         return pltpu.make_async_remote_copy(
             src_ref=part.at[pl.ds(pl.multiple_of(other * OWN, OWN), OWN), :], dst_ref=coef_buf.at[source],
-            send_sem=cr_send.at[other], recv_sem=cr_recv.at[source],
+            send_sem=cr_sem.at[0], recv_sem=cr_sem.at[1],
             device_id=(me, other), device_id_type=MESH)
 
     others(lambda r: cr_copy(band, chan_other(r)).start())
     coef_buf[band] = part[pl.ds(pl.multiple_of(band * OWN, OWN), OWN), :]
     misfit(CHUNKS - 1)
 
-    gains_out[...] = gain[:, :, :ANT]
+    for chunk in range(CHUNKS):
+        for unit in range(UNITS):
+            row, lane = chunk * CHK + unit // ACROSS * 8, unit % ACROSS * LANES
+            wide[:, row:row + 8, lane:lane + LANES] = gain[chunk, unit]
+    gains_out[...] = wide[:, :, :ANT]
     east = vec_acc[0:1, :] / vec_acc[2:3, :]
     north = vec_acc[1:2, :] / vec_acc[2:3, :]
     square[...] = jnp.zeros_like(square)
@@ -451,12 +459,12 @@
     my_groups = vec_t[pl.ds(pl.multiple_of(band * OWN, OWN), OWN), :]
 
     loads[7].wait()
-    others(lambda r: mod_copy(chan_other(r), band).wait_recv())
-    others(lambda r: mod_copy(band, chan_other(r)).wait_send())
+    arrivals(mod_sem.at[1], coef_buf.at[0:N - 1]).wait()
+    arrivals(mod_sem.at[0], coef_buf.at[0:N - 1]).wait()
     weights_east = model_band[...] * my_groups[:, 0:1]
     weights_north = model_band[...] * my_groups[:, 1:2]
 
-    others(lambda r: cr_copy(chan_other(r), band).wait_recv())
+    arrivals(cr_sem.at[1], coef_buf.at[0:N - 1]).wait()
     coef = coef_buf[0]
     for source in range(1, N):
         coef = coef + coef_buf[source]
@@ -477,13 +485,13 @@
     def band_copy(source, other):
         return pltpu.make_async_remote_copy(
             src_ref=band_send_buf.at[other], dst_ref=band_buf.at[source],
-            send_sem=band_send.at[other], recv_sem=band_recv.at[source],
+            send_sem=band_sem.at[0], recv_sem=band_sem.at[1],
             device_id=(me, other), device_id_type=MESH)
 
     others(lambda r: band_copy(band, chan_other(r)).start())
     band_buf[band] = band_send_buf[band]
-    others(lambda r: cr_copy(band, chan_other(r)).wait_send())
-    others(lambda r: band_copy(chan_other(r), band).wait_recv())
+    arrivals(cr_sem.at[0], coef_buf.at[0:N - 1]).wait()
+    arrivals(band_sem.at[1], coef_buf.at[0:N - 1]).wait()
     sums = band_buf[0]
     for source in range(1, N):
         sums = sums + band_buf[source]
@@ -494,16 +502,16 @@
     def tot_copy(source, other):
         return pltpu.make_async_remote_copy(
             src_ref=tot_buf.at[source], dst_ref=tot_buf.at[source],
-            send_sem=tot_send.at[other], recv_sem=tot_recv.at[source],
+            send_sem=tot_sem.at[0], recv_sem=tot_sem.at[1],
             device_id=(other, band), device_id_type=MESH)
 
     others(lambda r: tot_copy(me, grp_other(r)).start())
-    others(lambda r: band_copy(band, chan_other(r)).wait_send())
-    others(lambda r: tot_copy(grp_other(r), me).wait_recv())
+    arrivals(band_sem.at[0], coef_buf.at[0:N - 1]).wait()
+    arrivals(tot_sem.at[1], tot_buf.at[0:N - 1]).wait()
     totals = tot_buf[0]
     for source in range(1, N):
         totals = totals + tot_buf[source]
-    others(lambda r: tot_copy(me, grp_other(r)).wait_send())
+    arrivals(tot_sem.at[0], tot_buf.at[0:N - 1]).wait()
     chi_out[...] = totals[7:8, :CH]
 
     terms = jnp.sum(totals[8:16], axis=1, keepdims=True)
@@ -554,13 +562,14 @@
             pltpu.VMEM((6 * CHK, BL), bf16),
             pltpu.VMEM((6 * CHK, 2 * BL), bf16),
             pltpu.VMEM((STEPS, 2 * CHK, 2 * TILE), f32),
+            pltpu.VMEM((CHUNKS, UNITS, 2, 8, LANES), f32),
             pltpu.VMEM((2, CH, ANT_PAD), f32),
             pltpu.VMEM((4 * CHK, ANT_PAD), bf16),
             pltpu.VMEM((6 * CHK, GRP), f32),
             pltpu.VMEM((2, CH, GRP), f32),
             pltpu.VMEM((4 * CHK, GRP), bf16),
             pltpu.VMEM((6 * CHK, ANT_PAD), f32),
-            pltpu.VMEM((CHUNKS, 3, CHK, ANT_PAD), f32),
+            pltpu.VMEM((CHUNKS, UNITS, 3, 8, LANES), f32),
             pltpu.VMEM((CHUNKS, N, 3, 8, LANES), f32),
             pltpu.VMEM((2 * CH, GRP), f32),
             pltpu.VMEM((GRP, 2 * NDLY), f32),
@@ -576,7 +585,7 @@
             pltpu.VMEM((N, 16, LANES), f32),
             dma((7 + CHUNKS,)),
             dma((CHUNKS,)), dma((CHUNKS,)), dma((CHUNKS,)), dma((CHUNKS,)),
-        ] + [dma((N,))] * 8,
+        ] + [dma((2,))] * 4,
         compiler_params=pltpu.CompilerParams(
             collective_id=0, has_side_effects=True, vmem_limit_bytes=60 * 1024 * 1024),
         cost_estimate=pl.CostEstimate(flops=20_000_000_000, bytes_accessed=4_000_000, transcendentals=0),

time: 90 us -> 88.3 us (0.981)
  Pallas kernels: 84.8 us -> 83.2 us
    pallas_call x1, Pallas kernels: 84.8 us -> 83.2 us  [per_device(): pl.pallas_call(kernel, out_shape=(jax.ShapeDtypeStruct((2, CH, ANT), f32)...]
where the time goes in v5:
time: 88.3 us; the launch traced here: 88.2 us
  Pallas kernels  83.2 us (94%)
  local copies, waits for them, and re-layouts  4.35 us (5%)
    pallas_call x1, Pallas kernels, per_device(): pl.pallas_call(kernel, out_shape=(jax.ShapeDtypeStruct((2, CH, ANT), f32)...  83.2 us
    unnamed x3, local copies, waits for them, and re-layouts  4.35 us

profile of v5, /device:TPU:1, one launch (start us, length us, event | category | flops | bytes accessed | tf_op | source)
XLA Modules:
  0.0 88.2 jit_solution(15274771587376971632)
XLA Ops:
  0.6 83.2 %shard_map.103 = (f32[2,96,350]{2,1,0:T(8,128)}, f32[2,96,128]{2,1,0:T(8,128)}, f32[1,96]{1,0:T(1,128)}) custom-call(f32[2,96,2048]{2,1,0:T(8,128)} %vis_hbm.1, s32[2,2048]{1,0:T(2,128)} %ants_hbm.1, s32[1,2048]{1,0:T(1,128)} %gid_hbm.1, f32[2,96,128]{2,1,0:T(8,128)} %sky_hbm.1, f32[2,96,350]{2,1,0:T(8,128)} %start_hbm.1, f32[2,350]{1,0:T(2,128)} %coords_hbm.1, ...), custom_call_target="tpu_custom_call" | custom-call | flops 20000000000 | bytes 4000000 | tf_op jit(solution)/shard_map/pallas_call | solution.py:540
  83.8 1.7 %copy.14 = f32[2,96,350]{2,1,0:T(8,128)} copy(f32[2,96,350]{2,1,0:T(8,128)} %get-tuple-element.12) | data formatting | bytes 537600
  85.5 1.5 %copy.15 = f32[2,96,128]{2,1,0:T(8,128)} copy(f32[2,96,128]{2,1,0:T(8,128)} %get-tuple-element.13) | data formatting | bytes 196608
  87.1 1.1 %copy.16 = f32[96]{0:T(128)} copy(f32[96]{0:T(128)} %bitcast.1) | data formatting | bytes 768

commit v6 on v5

--- a/solution.py
+++ b/solution.py
@@ -531,6 +531,17 @@
     rotation_sin = jnp.sin(turn) * columns[:, 3:4]
     cal_out[0] = ur * rotation_cos + ui * rotation_sin
     cal_out[1] = ui * rotation_cos - ur * rotation_sin
+
+
+def store(gains, cal, chi, gains_out, cal_out, chi_out, sem):
+    copies = [
+        pltpu.make_async_copy(source, target, sem.at[place])
+        for place, (source, target) in enumerate(((gains, gains_out), (cal, cal_out), (chi, chi_out)))
+    ]
+    for copy in copies:
+        copy.start()
+    for copy in copies:
+        copy.wait()
 
 
 def per_device(ahead, back, vis, ants, gid, sky, start, coords):
@@ -590,6 +601,17 @@
             collective_id=0, has_side_effects=True, vmem_limit_bytes=60 * 1024 * 1024),
         cost_estimate=pl.CostEstimate(flops=20_000_000_000, bytes_accessed=4_000_000, transcendentals=0),
     )(vis, ants, gid, sky, start, coords, ahead, back)
+    gains, cal, chi = pl.pallas_call(
+        store,
+        out_shape=(
+            jax.ShapeDtypeStruct((2, CH, ANT), f32),
+            jax.ShapeDtypeStruct((2, CH, GRP), f32),
+            jax.ShapeDtypeStruct((1, CH), f32),
+        ),
+        in_specs=[vmem] * 3,
+        out_specs=(hbm, hbm, hbm),
+        scratch_shapes=[dma((3,))],
+    )(gains, cal, chi)
     return gains, cal, chi.reshape(CH)
 
 

time: 88.3 us -> 85.7 us (0.971)
  local copies, waits for them, and re-layouts: 4.35 us -> 0 us
  Pallas kernels: 83.2 us -> 84.9 us
    unnamed x3 -> x0, local copies, waits for them, and re-layouts: 4.35 us -> none
    pallas_call x0 -> x1, Pallas kernels: none -> 1.78 us  [per_device(): pl.pallas_call(store, out_shape=(jax.ShapeDtypeStruct((2, CH, ANT), f32),...]
where the time goes in v6:
time: 85.7 us; the launch traced here: 85.5 us
  Pallas kernels  84.9 us (99%)
    pallas_call x1, Pallas kernels, per_device(): pl.pallas_call(kernel, out_shape=(jax.ShapeDtypeStruct((2, CH, ANT), f32)...  83.1 us
    pallas_call x1, Pallas kernels, per_device(): pl.pallas_call(store, out_shape=(jax.ShapeDtypeStruct((2, CH, ANT), f32),...  1.78 us

profile of v6, /device:TPU:1, one launch (start us, length us, event | category | flops | bytes accessed | tf_op | source)
XLA Modules:
  0.0 85.5 jit_solution(1869378817587232583)
XLA Ops:
  0.6 83.1 %shard_map.103 = (f32[2,96,350]{2,1,0:T(8,128)}, f32[2,96,128]{2,1,0:T(8,128)}, f32[1,96]{1,0:T(1,128)}) custom-call(f32[2,96,2048]{2,1,0:T(8,128)} %vis_hbm.1, s32[2,2048]{1,0:T(2,128)} %ants_hbm.1, s32[1,2048]{1,0:T(1,128)} %gid_hbm.1, f32[2,96,128]{2,1,0:T(8,128)} %sky_hbm.1, f32[2,96,350]{2,1,0:T(8,128)} %start_hbm.1, f32[2,350]{1,0:T(2,128)} %coords_hbm.1, ...), custom_call_target="tpu_custom_call" | custom-call | flops 20000000000 | bytes 4000000 | tf_op jit(solution)/shard_map/pallas_call | solution.py:551
  83.7 1.8 %shard_map.104 = (f32[2,96,350]{2,1,0:T(8,128)}, f32[2,96,128]{2,1,0:T(8,128)}, f32[1,96]{1,0:T(1,128)}) custom-call(f32[2,96,350]{2,1,0:T(8,128)} %get-tuple-element.9.gains, f32[2,96,128]{2,1,0:T(8,128)} %get-tuple-element.10.cal, f32[1,96]{1,0:T(1,128)} %get-tuple-element.11.chi), custom_call_target="tpu_custom_call" | custom-call | tf_op jit(solution)/shard_map/pallas_call | solution.py:604

commit v7 on v6

--- a/solution.py
+++ b/solution.py
@@ -428,7 +428,9 @@
         for unit in range(UNITS):
             row, lane = chunk * CHK + unit // ACROSS * 8, unit % ACROSS * LANES
             wide[:, row:row + 8, lane:lane + LANES] = gain[chunk, unit]
-    gains_out[...] = wide[:, :, :ANT]
+    start[...] = wide[:, :, :ANT]
+    copy_gains = pltpu.make_async_copy(start, gains_out, load_sem.at[7 + CHUNKS])
+    copy_gains.start()
     east = vec_acc[0:1, :] / vec_acc[2:3, :]
     north = vec_acc[1:2, :] / vec_acc[2:3, :]
     square[...] = jnp.zeros_like(square)
@@ -531,6 +533,7 @@
     rotation_sin = jnp.sin(turn) * columns[:, 3:4]
     cal_out[0] = ur * rotation_cos + ui * rotation_sin
     cal_out[1] = ui * rotation_cos - ur * rotation_sin
+    copy_gains.wait()
 
 
 def store(gains, cal, chi, gains_out, cal_out, chi_out, sem):
@@ -556,7 +559,7 @@
             jax.ShapeDtypeStruct((1, CH), f32),
         ),
         in_specs=[hbm] * 8,
-        out_specs=(vmem, vmem, vmem),
+        out_specs=(hbm, vmem, vmem),
         scratch_shapes=[
             pltpu.VMEM((2, CH, BL), f32),
             pltpu.VMEM((2, BL), jnp.int32),
@@ -594,7 +597,7 @@
             pltpu.VMEM((N, 8, LANES), f32),
             pltpu.VMEM((N, 8, LANES), f32),
             pltpu.VMEM((N, 16, LANES), f32),
-            dma((7 + CHUNKS,)),
+            dma((8 + CHUNKS,)),
             dma((CHUNKS,)), dma((CHUNKS,)), dma((CHUNKS,)), dma((CHUNKS,)),
         ] + [dma((2,))] * 4,
         compiler_params=pltpu.CompilerParams(

time: 85.7 us -> 85.7 us (level)
  no operation moved by 1% of the time
where the time goes in v7:
time: 85.7 us; the launch traced here: 85.5 us
  Pallas kernels  84.9 us (99%)
    pallas_call x1, Pallas kernels, per_device(): pl.pallas_call(kernel, out_shape=(jax.ShapeDtypeStruct((2, CH, ANT), f32)...  83.1 us
    pallas_call x1, Pallas kernels, per_device(): pl.pallas_call(store, out_shape=(jax.ShapeDtypeStruct((2, CH, ANT), f32),...  1.78 us

profile of v7, /device:TPU:1, one launch (start us, length us, event | category | flops | bytes accessed | tf_op | source)
XLA Modules:
  0.0 85.5 jit_solution(17762058464883158170)
XLA Ops:
  0.6 83.1 %shard_map.103 = (f32[2,96,350]{2,1,0:T(8,128)}, f32[2,96,128]{2,1,0:T(8,128)}, f32[1,96]{1,0:T(1,128)}) custom-call(f32[2,96,2048]{2,1,0:T(8,128)} %vis_hbm.1, s32[2,2048]{1,0:T(2,128)} %ants_hbm.1, s32[1,2048]{1,0:T(1,128)} %gid_hbm.1, f32[2,96,128]{2,1,0:T(8,128)} %sky_hbm.1, f32[2,96,350]{2,1,0:T(8,128)} %start_hbm.1, f32[2,350]{1,0:T(2,128)} %coords_hbm.1, ...), custom_call_target="tpu_custom_call" | custom-call | flops 20000000000 | bytes 4000000 | tf_op jit(solution)/shard_map/pallas_call | solution.py:554
  83.7 1.8 %shard_map.104 = (f32[2,96,350]{2,1,0:T(8,128)}, f32[2,96,128]{2,1,0:T(8,128)}, f32[1,96]{1,0:T(1,128)}) custom-call(f32[2,96,350]{2,1,0:T(8,128)} %get-tuple-element.9.gains, f32[2,96,128]{2,1,0:T(8,128)} %get-tuple-element.10.cal, f32[1,96]{1,0:T(1,128)} %get-tuple-element.11.chi), custom_call_target="tpu_custom_call" | custom-call | tf_op jit(solution)/shard_map/pallas_call | solution.py:607
